TPU v7x, 256 devices: a whole 4x4x8 slice. The times are simulated.
256 devices in a mesh: row: 8 (over z_hi, core), col: 4 (over y), depth: 8 (over z_lo, x).
Axes of the slice: x: 4, y: 4, z: 8 (z_hi: 4, z_lo: 2; z = z_hi * 2 + z_lo), core: 2. Of those that a mesh axis runs over, the one named last changes fastest.
Arguments:
- tokens: bfloat16 [6144, 2560], P(('col', 'depth'), 'row'), may hold values from -6 to 6
- up_weight: bfloat16 [2560, 10240], P('col', 'row'), may hold values from -0.125 to 0.125
- up_bias: float32 [10240], P('row'), may hold values from -3 to 3
- down_weight: bfloat16 [10240, 2560], P('col', 'row'), may hold values from -0.0625 to 0.0625
- down_bias: float32 [2560], P('row'), may hold values from -3 to 3
- out_grad: bfloat16 [6144, 2560], P(('col', 'depth'), 'row'), may hold values from -6 to 6
Outputs:
- layer_out: bfloat16 [6144, 2560], P(('col', 'depth'), 'row')
- grad_in: bfloat16 [6144, 2560], P(('col', 'depth'), 'row')
- grad_up: bfloat16 [2560, 10240], P('col', 'row')
- grad_up_bias: bfloat16 [10240], P('row')
- grad_down: bfloat16 [10240, 2560], P('col', 'row')
- grad_down_bias: bfloat16 [2560], P('row')
All inputs are finite; a program needn't handle non-finite values.
Results may differ from a plain program's by a relative error of at most 0.029.
Values may be sent and summed in bfloat16 or wider, within the bound.
A program may use at most 128 MiB of HBM per device.

v0:
```python
import math

import jax
import jax.numpy as jnp
from jax import lax
from jax.sharding import PartitionSpec as P

GELU_C = math.sqrt(2.0 / math.pi)


def gelu_parts(hidden_pre):
    tanh_arg = GELU_C * (hidden_pre + 0.044715 * hidden_pre * hidden_pre * hidden_pre)
    tanh_val = jnp.tanh(tanh_arg)
    gelu_value = 0.5 * hidden_pre * (1.0 + tanh_val)
    gelu_slope = 0.5 * (1.0 + tanh_val) + 0.5 * hidden_pre * (
        1.0 - tanh_val * tanh_val
    ) * GELU_C * (1.0 + 3.0 * 0.044715 * hidden_pre * hidden_pre)
    return (gelu_value, gelu_slope)


def per_device(tokens, up_weight, up_bias, down_weight, down_bias, out_grad):
    token_rows = tokens.shape[0]
    token_total = token_rows * lax.axis_size("col") * lax.axis_size("depth")
    grad_scale = 1.0 / math.sqrt(token_total)
    full_tokens = lax.all_gather(tokens, "row", axis=1, tiled=True)
    split_tokens = lax.all_to_all(full_tokens, "col", split_axis=1, concat_axis=0, tiled=True)
    up_columns = lax.all_gather(up_weight, "col", axis=0, tiled=True)
    hidden_pre = jnp.dot(full_tokens, up_columns, preferred_element_type=jnp.float32) + up_bias
    gelu_value, gelu_slope = gelu_parts(hidden_pre)
    activ = gelu_value.astype(jnp.bfloat16)
    full_activ = lax.all_gather(activ, "row", axis=1, tiled=True)
    split_activ = lax.all_to_all(full_activ, "col", split_axis=1, concat_axis=0, tiled=True)
    down_columns = lax.all_gather(down_weight, "col", axis=0, tiled=True)
    out_pre = jnp.dot(full_activ, down_columns, preferred_element_type=jnp.float32) + down_bias
    layer_out = out_pre.astype(jnp.bfloat16)
    grad_rows = lax.all_gather(out_grad, "col", axis=0, tiled=True)
    partial_act = jnp.dot(out_grad, down_columns.T, preferred_element_type=jnp.float32)
    partial_act = partial_act.astype(jnp.bfloat16).astype(jnp.float32)
    d_act = lax.psum_scatter(
        partial_act.astype(jnp.bfloat16), "row", scatter_dimension=1, tiled=True
    ).astype(jnp.float32)
    d_hidden = (d_act * gelu_slope).astype(jnp.bfloat16)
    hidden_rows = lax.all_gather(d_hidden, "col", axis=0, tiled=True)
    partial_input = jnp.dot(d_hidden, up_columns.T, preferred_element_type=jnp.float32)
    partial_input = partial_input.astype(jnp.bfloat16).astype(jnp.float32)
    input_sum = lax.psum_scatter(
        partial_input.astype(jnp.bfloat16), "row", scatter_dimension=1, tiled=True
    )
    along_tokens = (((0,), (0,)), ((), ()))
    up_term = (
        lax.dot_general(split_tokens, hidden_rows, along_tokens, preferred_element_type=jnp.float32)
        * grad_scale
    )
    up_bias_term = jnp.sum(hidden_rows.astype(jnp.float32), axis=0) * grad_scale
    down_term = (
        lax.dot_general(split_activ, grad_rows, along_tokens, preferred_element_type=jnp.float32)
        * grad_scale
    )
    down_bias_term = jnp.sum(grad_rows.astype(jnp.float32), axis=0) * grad_scale
    summed = (
        lax.psum(up_term.astype(jnp.bfloat16), "depth").astype(jnp.float32),
        lax.psum(up_bias_term.astype(jnp.bfloat16), "depth").astype(jnp.float32),
        lax.psum(down_term.astype(jnp.bfloat16), "depth").astype(jnp.float32),
        lax.psum(down_bias_term.astype(jnp.bfloat16), "depth").astype(jnp.float32),
    )
    grad_up = summed[0].astype(jnp.bfloat16)
    grad_up_bias = summed[1].astype(jnp.bfloat16)
    grad_down = summed[2].astype(jnp.bfloat16)
    grad_down_bias = summed[3].astype(jnp.bfloat16)
    return (layer_out, input_sum, grad_up, grad_up_bias, grad_down, grad_down_bias)


def solution(mesh):
    return jax.shard_map(
        per_device,
        mesh=mesh,
        in_specs=(
            P(("col", "depth"), "row"),
            P("col", "row"),
            P("row"),
            P("col", "row"),
            P("row"),
            P(("col", "depth"), "row"),
        ),
        out_specs=(
            P(("col", "depth"), "row"),
            P(("col", "depth"), "row"),
            P("col", "row"),
            P("row"),
            P("col", "row"),
            P("row"),
        ),
        check_vma=False,
    )
```

profile of v0, /device:TPU:1, one launch (start us, length us, event | category | flops | bytes accessed | tf_op | source)
XLA Modules:
  0.0 494.7 jit_solution(4320000272212700458)
XLA Ops:
  8.7 75.4 %all-gather.10.cloned.1.call-done = bf16[10240,320]{0,1:T(8,128)(2,1)} async-done(((bf16[2560,320]{0,1:T(8,128)(2,1)}), bf16[10240,320]{0,1:T(8,128)(2,1)}) %all-gather.10.cloned.1.call-update) | async-done | bytes 6553616 | tf_op jit(solution)/shard_map/all_gather | solution.py:33
  84.1 7.0 %convolution_convert_fusion = bf16[192,10240]{1,0:T(8,128)(2,1)} fusion(bf16[192,320]{1,0:T(8,128)(2,1)} %param.11, bf16[10240,320]{0,1:T(8,128)(2,1)} %all-gather.10.cloned.1.call-done), kind=kOutput, calls=%fused_computation | convolution fusion | flops 1260257280 | bytes 10608640 | tf_op jit(solution)/shard_map/dot_general | solution.py:37
  91.1 0.8 copy-done.4
  92.0 21.8 %all-gather = bf16[8,320,192]{1,2,0:T(8,128)(2,1)S(1)} all-gather(bf16[1,320,192]{1,2,0:T(8,128)(2,1)S(1)} %bitcast.42), channel_id=1, replica_groups=mesh['row'=8,'col'=4,'depth'=8] {'row'}, dimensions={0}, use_global_device_ids=true | all-gather | bytes 1105920 | tf_op jit(solution)/shard_map/all_gather | solution.py:25
  115.3 41.8 %all-gather.6.cloned.1.call-done = bf16[2560,1280]{1,0:T(8,128)(2,1)} async-done(((bf16[640,1280]{1,0:T(8,128)(2,1)}), bf16[2560,1280]{1,0:T(8,128)(2,1)}) %all-gather.6.cloned.1.call-update) | async-done | bytes 6553616 | tf_op jit(solution)/shard_map/all_gather | solution.py:27
  157.1 59.0 %reduce-scatter.5.cloned.1.call-done = bf16[192,1280]{1,0:T(8,128)(2,1)} async-done(((bf16[192,10240]{1,0:T(8,128)(2,1)}), bf16[192,1280]{1,0:T(8,128)(2,1)}) %reduce-scatter.5.cloned.1.call-update) | async-done | bytes 491536 | tf_op jit(solution)/shard_map/reduce_scatter | solution.py:39
  216.1 5.8 %fusion.10 = (bf16[192,1280]{1,0:T(8,128)(2,1)}, bf16[192,1280]{1,0:T(8,128)(2,1)}) fusion(bf16[192,1280]{1,0:T(8,128)(2,1)} %reduce-scatter.5.cloned.1.call-done, f32[1280]{0:T(1024)S(1)} %copy-done.5, bf16[2560,192]{0,1:T(8,128)(2,1)S(1)} %reshape.21, bf16[2560,1280]{1,0:T(8,128)(2,1)} %all-gather.6.cloned.1.call-done), kind=kOutput, calls=%fused_computation.21 | convolution fusion | flops 1263943680 | bytes 9016320 | tf_op jit(solution)/shard_map/dot_general | solution.py:28
  222.5 1.0 copy.28
  223.5 4.1 all-to-all-start
  227.6 44.6 %all-gather.8.cloned.1.call-done = bf16[192,10240]{1,0:T(8,128)(2,1)} async-done(((bf16[192,1280]{1,0:T(8,128)(2,1)}), bf16[192,10240]{1,0:T(8,128)(2,1)}) %all-gather.8.cloned.1.call-update) | async-done | bytes 3932176 | tf_op jit(solution)/shard_map/all_gather | solution.py:31
  272.2 4.4 copy.27
  276.5 5.6 %all-to-all-start.1 = ((bf16[192,4,2560]{2,0,1:T(8,128)(2,1)}), bf16[192,4,2560]{2,0,1:T(8,128)(2,1)}, u32[]{:S(2)}, u32[]{:S(2)}) async-start(bf16[192,4,2560]{2,0,1:T(8,128)(2,1)} %bitcast.36), calls=%async_computation.2 | async-start | bytes 7864320 | tf_op jit(solution)/shard_map/all_to_all | solution.py:32
  282.1 5.2 %convolution_convert_fusion.1 = bf16[192,2560]{1,0:T(8,128)(2,1)S(1)} fusion(bf16[192,1280]{1,0:T(8,128)(2,1)S(1)} %copy-done.3, bf16[2560,1280]{1,0:T(8,128)(2,1)} %all-gather.6.cloned.1.call-done), kind=kOutput, calls=%fused_computation.6 | convolution fusion | flops 1258782720 | bytes 8028160 | tf_op jit(solution)/shard_map/dot_general | solution.py:44
  287.3 1.4 copy.21
  288.8 62.5 %all_gather.23 = bf16[768,320]{1,0:T(8,128)(2,1)S(1)} all-gather(bf16[192,320]{1,0:T(8,128)(2,1)S(1)} %copy-done.2), channel_id=1, replica_groups=mesh['row'=8,'col'=4,'depth'=8] {'col'}, dimensions={0}, use_global_device_ids=true | all-gather | bytes 614400 | tf_op jit(solution)/shard_map/all_gather | solution.py:36
  351.3 4.5 fusion.2
  355.8 4.8 fusion
  360.7 22.4 %reduce-scatter.7.cloned.1.call-done = bf16[320,192]{1,0:T(8,128)(2,1)} async-done(((bf16[2560,192]{1,0:T(8,128)(2,1)}), bf16[320,192]{1,0:T(8,128)(2,1)}) %reduce-scatter.7.cloned.1.call-update) | async-done | bytes 122896
  383.1 1.7 copy.22
  385.2 15.6 %all-reduce = (bf16[1280]{0:T(1024)(128)(2,1)}, bf16[320]{0:T(512)(128)(2,1)}) all-reduce(bf16[1280]{0:T(1024)(128)(2,1)S(1)} %multiply_convert_fusion.1, bf16[320]{0:T(512)(128)(2,1)S(1)} %multiply_convert_fusion.2), channel_id=1, replica_groups=mesh['row'=8,'col'=4,'depth'=8] {'depth'}, use_global_device_ids=true, to_apply=%region_4.0 | all-reduce | flops 1600 | bytes 6400 | tf_op jit(solution)/shard_map/psum | solution.py:62
  400.8 7.5 %fusion.3 = bf16[192,320]{1,0:T(8,128)(2,1)} fusion(bf16[192,10240]{1,0:T(8,128)(2,1)} %all-gather.8.cloned.1.call-done, bf16[10240,320]{0,1:T(8,128)(2,1)} %all-gather.10.cloned.1.call-done, f32[320]{0:T(512)S(1)} %copy-done.6), kind=kOutput, calls=%fused_computation.14 | convolution fusion | flops 1258414080 | bytes 10609920 | tf_op jit(solution)/shard_map/dot_general | solution.py:34
  408.2 74.8 %all-reduce.4.cloned.1.call-done = (bf16[640,1280]{0,1:T(8,128)(2,1)}, bf16[2560,320]{0,1:T(8,128)(2,1)}) async-done(((bf16[640,1280]{0,1:T(8,128)(2,1)}, bf16[2560,320]{0,1:T(8,128)(2,1)}), (bf16[640,1280]{0,1:T(8,128)(2,1)}, bf16[2560,320]{0,1:T(8,128)(2,1)})) %all-reduce.4.cloned.1.call-update) | async-done | bytes 3276816 | tf_op jit(solution)/shard_map/psum | solution.py:61
  483.0 3.7 copy.20
  486.7 1.2 copy.31
  (36 shorter events, 4.2 us)
Async XLA Ops:
  7.2 76.9 %all-gather.10.cloned.1.call-start = ((), (), s32[]{:S(2)}) async-start(), calls=%async_computation.6 | async-start | bytes 8192000 | tf_op jit(solution)/shard_map/all_gather | solution.py:33
  7.9 149.2 %all-gather.6.cloned.1.call-start = ((), (), s32[]{:S(2)}) async-start(), calls=%async_computation.4 | async-start | bytes 8192000 | tf_op jit(solution)/shard_map/all_gather | solution.py:27
  8.6 207.4 %reduce-scatter.5.cloned.1.call-start = ((), (), s32[]{:S(2)}) async-start(), calls=%async_computation.7 | async-start | bytes 4423680 | tf_op jit(solution)/shard_map/reduce_scatter | solution.py:39
  91.1 0.9 copy-start.4
  91.1 125.0 %copy-start.5 = (f32[1280]{0:T(1024)S(1)}, f32[1280]{0:T(1024)}, u32[]{:S(2)}) copy-start(f32[1280]{0:T(1024)} %param.8) | copy-start | bytes 15364
  91.1 181.1 %all-gather.8.cloned.1.call-start = ((), (), s32[]{:S(2)}) async-start(), calls=%async_computation.5 | async-start | bytes 4423680 | tf_op jit(solution)/shard_map/all_gather | solution.py:31
  221.9 129.4 %all-gather.12.cloned.1.call-start = ((), (), s32[]{:S(2)}) async-start(), calls=%async_computation.8 | async-start | bytes 2457600 | tf_op jit(solution)/shard_map/all_gather | solution.py:43
  223.5 53.0 %all-to-all-start = ((bf16[192,4,640]{2,0,1:T(8,128)(2,1)}), bf16[192,4,640]{2,0,1:T(8,128)(2,1)S(1)}, u32[]{:S(2)}, u32[]{:S(2)}) async-start(bf16[192,4,640]{2,0,1:T(8,128)(2,1)} %bitcast.35), calls=%async_computation.1 | async-start | bytes 1966080 | tf_op jit(solution)/shard_map/all_to_all | solution.py:26
  276.5 5.6 %copy-start.3 = (bf16[192,1280]{1,0:T(8,128)(2,1)S(1)}, bf16[192,1280]{1,0:T(8,128)(2,1)}, u32[]{:S(2)}) copy-start(bf16[192,1280]{1,0:T(8,128)(2,1)} %get-tuple-element.28) | copy-start | bytes 1474564
  276.5 79.3 %all-to-all-start.1 = ((bf16[192,4,2560]{2,0,1:T(8,128)(2,1)}), bf16[192,4,2560]{2,0,1:T(8,128)(2,1)}, u32[]{:S(2)}, u32[]{:S(2)}) async-start(bf16[192,4,2560]{2,0,1:T(8,128)(2,1)} %bitcast.36), calls=%async_computation.2 | async-start | bytes 7864320 | tf_op jit(solution)/shard_map/all_to_all | solution.py:32
  282.1 6.7 %copy-start.2 = (bf16[192,320]{1,0:T(8,128)(2,1)S(1)}, bf16[192,320]{1,0:T(8,128)(2,1)}, u32[]{:S(2)}) copy-start(bf16[192,320]{1,0:T(8,128)(2,1)} %param.11) | copy-start | bytes 368644
  282.1 101.0 %reduce-scatter.7.cloned.1.call-start = ((), (), s32[]{:S(2)}) async-start(), calls=%async_computation.9 | async-start | bytes 1474560
  288.8 194.2 %all-reduce.4.cloned.1.call-start = ((), (), s32[]{:S(2)}) async-start(), calls=%async_computation.10 | async-start | bytes 6553600 | tf_op jit(solution)/shard_map/psum | solution.py:61
  360.6 24.3 %copy-start = (bf16[768,1280]{1,0:T(8,128)(2,1)S(1)}, bf16[768,1280]{1,0:T(8,128)(2,1)}, u32[]{:S(2)}) copy-start(bf16[768,1280]{1,0:T(8,128)(2,1)} %all-gather.12.cloned.1.call-done) | copy-start | bytes 5898244
  360.6 40.2 %copy-start.6 = (f32[320]{0:T(512)S(1)}, f32[320]{0:T(512)}, u32[]{:S(2)}) copy-start(f32[320]{0:T(512)} %param.10) | copy-start | bytes 3844
  483.0 3.7 copy-start.1
Sparse Core Ops, SparseCore 0:
  9.8 74.2 all-gather.9
  85.9 71.1 all-gather.5
  159.6 56.3 reduce-scatter.4
  222.0 50.0 all-gather.7
  274.4 47.6 all-gather.11
  324.5 58.5 reduce-scatter.6
  386.4 96.5 all-reduce.3
where the time goes:
time: 495 us
  waiting for transfers between devices  320 us (65%)
  blocking collectives  100 us (20%)
  matrix products  34.7 us (7%)
  local copies, waits for them, and re-layouts  15.7 us (3%)
  between operations  14.2 us (3%)
  starting transfers between devices  9.89 us (2%)
    all_gather x1, waiting for transfers between devices, per_device(): down_columns = lax.all_gather(down_weight, 'col', axis=0, tiled=True)  75.4 us
    psum x1, waiting for transfers between devices, per_device(): lax.psum(up_term.astype(jnp.bfloat16), 'depth').astype(jnp.float32)  74.8 us
    all_gather x1, blocking collectives, per_device(): grad_rows = lax.all_gather(out_grad, 'col', axis=0, tiled=True)  62.5 us
    reduce_scatter x1, waiting for transfers between devices, per_device(): lax.psum_scatter(partial_act.astype(jnp.bfloat16), 'row', scatter_dimensi...  59 us
    all_gather x1, waiting for transfers between devices, per_device(): full_activ = lax.all_gather(activ, 'row', axis=1, tiled=True)  44.6 us
    all_gather x1, waiting for transfers between devices, per_device(): up_columns = lax.all_gather(up_weight, 'col', axis=0, tiled=True)  41.8 us
    unnamed x8, waiting for transfers between devices  24.4 us
    all_gather x1, blocking collectives, per_device(): full_tokens = lax.all_gather(tokens, 'row', axis=1, tiled=True)  21.8 us
  transfers between devices with their start and end apart: 9, of which 6 were waited for; matrix products, arithmetic and copies ran while one was open for 8% of the time, Pallas kernels for 0%

commit v1 on v0

v1 whole, which is shorter than its diff:
```python
import math

import jax
import jax.numpy as jnp
from jax import lax
from jax.experimental import pallas as pl
from jax.experimental.pallas import tpu as pltpu
from jax.sharding import PartitionSpec as P

GELU_C = math.sqrt(2.0 / math.pi)
MESH = pl.DeviceIdType.MESH
F32 = jnp.float32
BF16 = jnp.bfloat16
N_SEMS = 320


def gelu_parts(v):
    t = jnp.tanh(GELU_C * (v + 0.044715 * v * v * v))
    value = 0.5 * v * (1.0 + t)
    slope = 0.5 * (1.0 + t) + 0.5 * v * (1.0 - t * t) * GELU_C * (1.0 + 3.0 * 0.044715 * v * v)
    return value, slope


def nn(a, b):
    return lax.dot_general(a, b, (((1,), (0,)), ((), ())), preferred_element_type=F32)


def nt(a, b):
    return lax.dot_general(a, b, (((1,), (1,)), ((), ())), preferred_element_type=F32)


def rows(start, size, tile=16):
    return pl.ds(pl.multiple_of(start, tile), size)


def kernel(
    scale,
    tok, wu_in, bu_in, wd_in, bd_in, grad,
    o_out, gi_out, gu_out, gd_out, bu_out, bd_out,
    xr, piece, wdo, wdr, wdq, bb, bbr,
    full, wts, full_t,
    hps, hpr, hpo, slope, act, act_t, dps, dpr, dhid,
    part, ra, rb, xsum, zr, osend, orecv,
    gpart, ga, gb, gsum, gz, gfin, rd, rdo, rds,
    bt, br, yb, pb,
    sems,
):
    row, y, dep = lax.axis_index("row"), lax.axis_index("col"), lax.axis_index("depth")
    h, k = row // 2, lax.rem(row, 2)
    zl, x = dep // 4, lax.rem(dep, 4)
    dd = x * 2 + zl
    hh = h // 2
    hi = lax.rem(h, 2)

    def at(h_, k_, y_):
        return (h_ * 2 + k_, y_, dep)

    def dep_at(a, b):
        return (row, y, lax.rem(zl + b, 2) * 4 + lax.rem(x + a, 4))

    def y_at(a):
        return (row, lax.rem(y + a, 4), dep)

    partner = (h * 2 + 1 - k, y, dep)
    zpeer = dep_at(0, 1)

    bar = pltpu.get_barrier_semaphore()
    fixed = [partner] + [y_at(a) for a in (1, 2, 3)]
    fixed += [dep_at(a, b) for a in range(4) for b in range(2) if (a, b) != (0, 0)]
    for target in fixed:
        pl.semaphore_signal(bar, inc=1, device_id=target, device_id_type=MESH)
    count = len(fixed)

    def greet(h_, k_, y_):
        other = jnp.logical_not((h_ == h) & (k_ == k) & (y_ == y))

        @pl.when(other)
        def _():
            pl.semaphore_signal(bar, inc=1, device_id=at(h_, k_, y_), device_id_type=MESH)

        return other.astype(jnp.int32)

    for a in range(4):
        count = count + greet(a, hh, y)
    for a in range(2):
        for b in range(2):
            count = count + greet(2 * k + a, b, y)
    for j in range(2):
        count = count + greet(h, y // 2, 2 * k + j)
        count = count + greet(y, hh, 2 * k + j)
        count = count + greet(2 * k + j, y // 2, h)
    pl.semaphore_wait(bar, count)

    used = [0]
    sent = []

    def new(n=1):
        first = used[0]
        used[0] += n
        return first

    def send(src, dst, rsem, target):
        copy = pltpu.make_async_remote_copy(
            src_ref=src, dst_ref=dst, send_sem=sems.at[new()], recv_sem=sems.at[rsem],
            device_id=target, device_id_type=MESH,
        )
        copy.start()
        sent.append((copy, None))

    def send_maybe(src, dst, rsem, h_, k_, y_):
        mine = (h_ == h) & (k_ == k) & (y_ == y)
        copy = pltpu.make_async_remote_copy(
            src_ref=src, dst_ref=dst, send_sem=sems.at[new()], recv_sem=sems.at[rsem],
            device_id=at(h_, k_, y_), device_id_type=MESH,
        )

        @pl.when(jnp.logical_not(mine))
        def _():
            copy.start()

        @pl.when(mine)
        def _():
            pltpu.make_async_copy(src, dst, sems.at[rsem]).start()

        sent.append((copy, jnp.logical_not(mine)))

    def got(dst, rsem):
        pltpu.make_async_copy(dst, dst, sems.at[rsem]).wait()

    def ring(axis):
        if axis == "y":
            return y, y_at(1), y_at(3)
        return x, dep_at(1, 0), dep_at(3, 0)

    class Gather:
        def __init__(self, buf, size, axis):
            self.p, self.right, self.left = ring(axis)
            self.view = lambda i, q: buf.at[i, rows(lax.rem(q, 4) * size, size)]
            self.s_right = new(2)
            self.s_left = new(2)
            self.s_fwd = new(2)

        def first(self, i):
            mine = self.view(i, self.p)
            pair = [(self.s_right + i, self.right), (self.s_left + i, self.left)]
            for sem, target in pair if i == 0 else pair[::-1]:
                send(mine, mine, sem, target)

        def forward(self, i):
            if i == 0:
                block = self.view(0, self.p + 3)
                got(block, self.s_right)
                send(block, block, self.s_fwd, self.right)
            else:
                block = self.view(1, self.p + 1)
                got(block, self.s_left + 1)
                send(block, block, self.s_fwd + 1, self.left)

        def finish(self):
            got(self.view(1, self.p + 3), self.s_right + 1)
            got(self.view(0, self.p + 1), self.s_left)
            got(self.view(0, self.p + 2), self.s_fwd)
            got(self.view(1, self.p + 2), self.s_fwd + 1)

    class Reduce:
        def __init__(self, buf, first, second, size, axis):
            self.p, self.right, self.left = ring(axis)
            self.view = lambda i, q: buf.at[i, rows(lax.rem(q, 4) * size, size)]
            self.first, self.second = first, second
            self.s1, self.s2 = new(2), new(4)

        def far(self):
            send(self.view(0, self.p + 2), self.first.at[0], self.s1, self.right)
            send(self.view(1, self.p + 2), self.first.at[1], self.s1 + 1, self.left)

        def near(self):
            send(self.view(1, self.p + 1), self.second.at[0, 1], self.s2 + 1, self.right)
            send(self.view(0, self.p + 3), self.second.at[1, 0], self.s2 + 2, self.left)

        def middle(self):
            for i, q, target in ((0, self.p + 1, self.right), (1, self.p + 3, self.left)):
                got(self.first.at[i], self.s1 + i)
                block = self.view(i, q)
                block[...] = (block[...].astype(F32) + self.first[i].astype(F32)).astype(BF16)
                send(block, self.second.at[i, i], self.s2 + 3 * i, target)

        def total(self, i):
            got(self.second.at[0, i], self.s2 + i)
            got(self.second.at[1, i], self.s2 + 2 + i)
            return (
                self.view(i, self.p)[...].astype(F32)
                + self.second[0, i].astype(F32)
                + self.second[1, i].astype(F32)
            )

    def pair_lanes(own, other):
        first = jnp.where(k == 0, own, other).astype(F32)
        second = jnp.where(k == 0, other, own).astype(F32)
        return jnp.concatenate([first, second], axis=1).astype(BF16)

    def split_lanes(both):
        low, high = both[:, :320], both[:, 320:]
        return jnp.where(k == 0, low, high), jnp.where(k == 0, high, low)

    s_x = new(2)
    for n, src in enumerate((tok, grad)):
        send(src.at[rows((1 - k) * 96, 96)], xr.at[n], s_x + n, partner)
    s_wu = new(2)
    for j in range(2):
        send_maybe(
            wu_in.at[rows(dd * 80, 80), pl.ds(j * 640, 640)],
            wts.at[0, lax.rem(y, 2), rows(dd * 80, 80)],
            s_wu + lax.rem(y, 2), h, y // 2, 2 * k + j,
        )
    s_wd = new(1)
    send(wd_in.at[pl.ds(2 * (1 - k), 2), rows(dd * 80, 80)], wdr, s_wd, partner)
    s_wo = new(1)
    own_wd = pltpu.make_async_copy(wd_in.at[pl.ds(2 * k, 2), rows(dd * 80, 80)], wdo, sems.at[s_wo])
    own_wd.start()
    bb[...] = jnp.broadcast_to(bu_in[...], bb.shape)
    s_bb = new(1)
    send(bb, bbr, s_bb, partner)

    s_piece = [new(4), new(4)]

    def send_piece(n, src):
        got(xr.at[n], s_x + n)
        piece[n] = pair_lanes(src[rows(k * 96, 96), :], xr[n])
        for a in range(4):
            hz = lax.rem(h + a, 4)
            send_maybe(
                piece.at[n],
                full.at[n, hi, rows(y * 192 + k * 96, 96)],
                s_piece[n] + hi * 2 + k, hz, hh, y,
            )

    def got_pieces(n, i):
        for kk in range(2):
            got(full.at[n, i, rows(y * 192 + kk * 96, 96)], s_piece[n] + i * 2 + kk)

    send_piece(0, tok)

    own_wd.wait()
    got(wdr, s_wd)
    s_wd2 = new(2)
    for j in range(2):
        wdq[j] = pair_lanes(wdo[j], wdr[j])
    for j in range(2):
        send_maybe(
            wdq.at[j], wts.at[1, hi, rows(dd * 80, 80)], s_wd2 + hi, y, hh, 2 * k + j,
        )
    send_piece(1, grad)

    s_zl = new(2)

    def over_zl(n):
        mine = wts.at[n, :, rows(dd * 80, 80)]
        for i in range(2):
            got(wts.at[n, i, rows(dd * 80, 80)], (s_wu if n == 0 else s_wd2) + i)
        send(mine, mine, s_zl + n, zpeer)

    def got_zl(n):
        got(wts.at[n, :, rows((x * 2 + 1 - zl) * 80, 80)], s_zl + n)

    wag = [Gather(wts.at[n], 160, "x") for n in range(2)]
    tag = [Gather(full.at[n], 192, "y") for n in range(2)]

    over_zl(0)
    for i in range(2):
        got_pieces(0, i)
        tag[0].first(i)
    got_zl(0)
    for i in range(2):
        wag[0].first(i)
    over_zl(1)
    for i in range(2):
        tag[0].forward(i)
    for i in range(2):
        wag[0].forward(i)
    got_zl(1)
    for i in range(2):
        wag[1].first(i)
    for i in range(2):
        got_pieces(1, i)
        tag[1].first(i)

    half = 384
    own_rows = rows(k * half, half)
    other_rows = rows((1 - k) * half, half)
    tag[0].finish()
    for i in range(2):
        full_t[i] = full[0, i].T
    wag[0].finish()
    for i in range(2):
        tag[1].forward(i)
    for i in range(2):
        wag[1].forward(i)
    s_hp, s_act, s_dp, s_dh = new(1), new(1), new(1), new(1)
    hps[...] = nn(full[0, 0, other_rows], wts[0, 0]) + nn(full[0, 1, other_rows], wts[0, 1])
    send(hps, hpr, s_hp, partner)
    hpo[...] = nn(full[0, 0, own_rows], wts[0, 0]) + nn(full[0, 1, own_rows], wts[0, 1])
    got(bbr, s_bb)
    low = jnp.where(k == y // 2, bb[0:1], bbr[0:1])
    bias = jnp.where(lax.rem(y, 2) == 0, low[:, :640], low[:, 640:])
    got(hpr, s_hp)
    value, slope_now = gelu_parts(hpo[...] + hpr[...] + bias)
    slope[...] = slope_now
    act[own_rows] = value.astype(BF16)
    send(act.at[own_rows], act.at[own_rows], s_act, partner)

    tag[1].finish()
    wag[1].finish()
    dps[...] = nt(full[1, 0, other_rows], wts[1, 0]) + nt(full[1, 1, other_rows], wts[1, 1])
    send(dps, dpr, s_dp, partner)
    got(act.at[other_rows], s_act)
    act_t[...] = act[...].T

    ored = [Reduce(part.at[n], ra.at[n], rb.at[n], 192, "y") for n in range(2)]
    gred = [Reduce(gpart.at[n], ga.at[n], gb.at[n], 160, "x") for n in range(2)]

    def out_block(n, q):
        block = rows(lax.rem(q, 4) * 192, 192)
        for i in range(2):
            if n == 0:
                part[0, i, block] = nn(act[block], wts[1, i]).astype(BF16)
            else:
                part[1, i, block] = nt(dhid[block], wts[0, i]).astype(BF16)

    def grad_block(n, q):
        block = rows(lax.rem(q, 4) * 160, 160)
        for i in range(2):
            if n == 0:
                term = nn(full_t[i, block], dhid[...])
            else:
                term = nn(act_t[block], full[1, i])
            gpart[n, i, block] = (term * scale).astype(BF16)

    out_block(0, y + 2)
    ored[0].far()
    grad_block(1, x + 2)
    gred[1].far()
    out_block(0, y + 1)
    out_block(0, y + 3)
    ored[0].near()
    grad_block(1, x + 1)
    grad_block(1, x + 3)
    gred[1].near()
    got(dpr, s_dp)
    d_own = nt(full[1, 0, own_rows], wts[1, 0]) + nt(full[1, 1, own_rows], wts[1, 1])
    dhid[own_rows] = ((d_own + dpr[...]) * slope[...]).astype(BF16)
    send(dhid.at[own_rows], dhid.at[own_rows], s_dh, partner)
    ored[0].middle()
    gred[1].middle()
    got(dhid.at[other_rows], s_dh)
    out_block(1, y + 2)
    ored[1].far()
    grad_block(0, x + 2)
    gred[0].far()
    out_block(1, y + 1)
    out_block(1, y + 3)
    ored[1].near()
    grad_block(0, x + 1)
    grad_block(0, x + 3)
    gred[0].near()
    out_block(0, y)
    grad_block(1, x)

    ones = jnp.ones((16, 768), BF16)
    terms = [nn(ones, dhid[...]), nn(ones, full[1, 0]), nn(ones, full[1, 1])]
    bt[...] = jnp.zeros_like(bt)
    for n in range(15):
        term = terms[n // 5][0:1, (n % 5) * 128 : (n % 5 + 1) * 128] * scale
        bt[n : n + 1] = term.astype(BF16).astype(F32)
    s_bt = new(8)
    for a in range(4):
        for b in range(2):
            if (a, b) != (0, 0):
                n = a * 2 + b
                send(bt, br.at[n], s_bt + n, dep_at(a, b))

    s_oz = [new(4), new(4)]

    def out_z(n):
        for i in range(2):
            xsum[n, i] = ored[n].total(i).astype(BF16)
            for kk in range(2):
                send_maybe(
                    xsum.at[n, i, pl.ds(kk * 96, 96)], zr.at[n, h], s_oz[n] + h, 2 * k + i, kk, y
                )

    s_gz, s_gr = [new(1), new(1)], [new(2), new(2)]

    def grad_zl(n):
        for i in range(2):
            gsum[n, i] = gred[n].total(i)
        gz[n, 0] = gsum[n, :, rows((1 - zl) * 80, 80)].astype(BF16)
        send(gz.at[n, 0], gz.at[n, 1], s_gz[n], zpeer)

    def grad_home(n):
        got(gz.at[n, 1], s_gz[n])
        gfin[n] = (gsum[n, :, rows(zl * 80, 80)] + gz[n, 1].astype(F32)).astype(BF16)
        for i in range(2):
            if n == 0:
                send_maybe(
                    gfin.at[0, i],
                    gu_out.at[rows(dd * 80, 80), pl.ds(pl.multiple_of(lax.rem(y, 2) * 640, 128), 640)],
                    s_gr[0] + lax.rem(y, 2), h, y // 2, 2 * k + i,
                )
            else:
                send_maybe(
                    gfin.at[1, i], rd.at[lax.rem(y, 2)], s_gr[1] + lax.rem(y, 2), 2 * k + i, y // 2, h
                )

    grad_zl(1)
    ored[1].middle()
    gred[0].middle()
    grad_home(1)
    out_block(1, y)
    grad_block(0, x)
    out_z(0)

    s_rd = new(1)
    s_gzl = [new(1), new(1)]
    for j in range(2):
        got(rd.at[j], s_gr[1] + j)
        mine, theirs = split_lanes(rd[j].astype(F32))
        gd_out[2 * k + j, rows(dd * 80, 80)] = mine.astype(BF16)
        rds[j] = theirs.astype(BF16)
    send(rds, rdo, s_rd, partner)
    got(rdo, s_rd)
    for j in range(2):
        gd_out[2 * (1 - k) + j, rows(dd * 80, 80)] = rdo[j]

    def grad_views(n):
        if n == 0:
            return lambda i, start, size: gu_out.at[rows(start, size), pl.ds(i * 640, 640)]
        return lambda i, start, size: gd_out.at[pl.ds(i * 2, 2), rows(start, size)]

    def back_zl(n):
        view = grad_views(n)
        for i in range(2):
            mine = view(i, dd * 80, 80)
            send(mine, mine, s_gb[n] + i, zpeer)

    class GatherBack(Gather):
        def __init__(self, n):
            self.p, self.right, self.left = ring("x")
            view = grad_views(n)
            self.view = lambda i, q: view(i, lax.rem(q, 4) * 160, 160)
            self.s_right, self.s_left, self.s_fwd = new(2), new(2), new(2)

    def back_first(n):
        view = grad_views(n)
        for i in range(2):
            got(view(i, (x * 2 + 1 - zl) * 80, 80), s_gb[n] + i)
            back[n].first(i)

    s_gb = [new(2), new(2)]
    back = [GatherBack(n) for n in range(2)]
    back_zl(1)
    grad_zl(0)
    grad_home(0)
    back_first(1)
    for i in range(2):
        got(gu_out.at[rows(dd * 80, 80), pl.ds(i * 640, 640)], s_gr[0] + i)
    back_zl(0)
    for i in range(2):
        back[1].forward(i)
    out_z(1)
    back_first(0)

    total = bt[...]
    for n in range(1, 8):
        got(br.at[n], s_bt + n)
        total = total + br[n]
    yb[y] = total
    s_yb = new(4)
    for a in range(1, 4):
        send(yb.at[y], yb.at[y], s_yb + a, y_at(a))
    s_pb = new(1)
    send(yb.at[y], pb, s_pb, partner)

    s_of = [new(1), new(1)]
    for n in range(2):
        total = jnp.zeros((96, 640), F32)
        for a in range(4):
            got(zr.at[n, a], s_oz[n] + a)
            total = total + zr[n, a].astype(F32)
        mine, theirs = split_lanes(total)
        osend[n] = theirs
        send(osend.at[n], orecv.at[n], s_of[n], partner)
        if n == 0:
            o_out[rows(k * 96, 96)] = (mine + bd_in[...]).astype(BF16)
        else:
            gi_out[rows(k * 96, 96)] = mine.astype(BF16)
    got(orecv.at[0], s_of[0])
    o_out[rows((1 - k) * 96, 96)] = (orecv[0] + bd_in[...]).astype(BF16)
    got(orecv.at[1], s_of[1])
    gi_out[rows((1 - k) * 96, 96)] = orecv[1].astype(BF16)

    for i in range(2):
        back[0].forward(i)
    for a in range(1, 4):
        got(yb.at[lax.rem(y + 4 - a, 4)], s_yb + a)
    got(pb, s_pb)
    bu_out[0:5] = yb[2 * k][0:5]
    bu_out[5:10] = yb[2 * k + 1][0:5]
    bd_out[0:10] = jnp.where(k == hh, yb[y][5:15], pb[5:15])
    back[1].finish()
    back[0].finish()

    for copy, when in sent:
        if when is None:
            copy.wait_send()
        else:

            @pl.when(when)
            def _(copy=copy):
                copy.wait_send()

    assert used[0] <= N_SEMS, used[0]


def per_device(tokens, up_weight, up_bias, down_weight, down_bias, out_grad):
    token_rows = tokens.shape[0]
    scale = 1.0 / math.sqrt(token_rows * lax.axis_size("col") * lax.axis_size("depth"))
    vmem = pl.BlockSpec(memory_space=pltpu.VMEM)
    hbm = pl.BlockSpec(memory_space=pl.ANY)
    scratch = [
        ((2, 96, 320), BF16),
        ((2, 96, 640), BF16),
        ((2, 80, 320), BF16),
        ((2, 80, 320), BF16),
        ((2, 80, 640), BF16),
        ((8, 1280), F32),
        ((8, 1280), F32),
        ((2, 2, 768, 640), BF16),
        ((2, 2, 640, 640), BF16),
        ((2, 640, 768), BF16),
        ((384, 640), F32),
        ((384, 640), F32),
        ((384, 640), F32),
        ((384, 640), F32),
        ((768, 640), BF16),
        ((640, 768), BF16),
        ((384, 640), F32),
        ((384, 640), F32),
        ((768, 640), BF16),
        ((2, 2, 768, 640), BF16),
        ((2, 2, 192, 640), BF16),
        ((2, 2, 2, 192, 640), BF16),
        ((2, 2, 192, 640), BF16),
        ((2, 4, 96, 640), BF16),
        ((2, 96, 320), F32),
        ((2, 96, 320), F32),
        ((2, 2, 640, 640), BF16),
        ((2, 2, 160, 640), BF16),
        ((2, 2, 2, 160, 640), BF16),
        ((2, 2, 160, 640), F32),
        ((2, 2, 2, 80, 640), BF16),
        ((2, 2, 80, 640), BF16),
        ((2, 80, 640), BF16),
        ((2, 80, 320), BF16),
        ((2, 80, 320), BF16),
        ((16, 128), F32),
        ((8, 16, 128), F32),
        ((4, 16, 128), F32),
        ((16, 128), F32),
    ]
    out = pl.pallas_call(
        lambda *refs: kernel(scale, *refs),
        name="mlp_block",
        out_shape=[
            jax.ShapeDtypeStruct((192, 320), BF16),
            jax.ShapeDtypeStruct((192, 320), BF16),
            jax.ShapeDtypeStruct((640, 1280), BF16),
            jax.ShapeDtypeStruct((4, 640, 320), BF16),
            jax.ShapeDtypeStruct((16, 128), F32),
            jax.ShapeDtypeStruct((16, 128), F32),
        ],
        in_specs=[vmem, hbm, vmem, hbm, vmem, vmem],
        out_specs=[vmem] * 6,
        scratch_shapes=[pltpu.VMEM(*s) for s in scratch] + [pltpu.SemaphoreType.DMA((N_SEMS,))],
        compiler_params=pltpu.CompilerParams(
            collective_id=0, has_side_effects=True, vmem_limit_bytes=56 << 20
        ),
        cost_estimate=pl.CostEstimate(
            flops=6 * 2 * 768 * 1280 * 640, bytes_accessed=12 << 20, transcendentals=384 * 640
        ),
    )(
        tokens,
        up_weight,
        up_bias.reshape(1, 1280),
        down_weight.reshape(4, 640, 320),
        down_bias.reshape(1, 320),
        out_grad,
    )
    layer_out, grad_in, grad_up, grad_down, bu, bd = out
    row = lax.axis_index("row")
    grad_up_bias = bu[:10].reshape(1280).astype(BF16)
    start = lax.rem(row // 2, 2) * 640 + lax.rem(row, 2) * 320
    grad_down_bias = lax.dynamic_slice(bd[:10].reshape(1280), (start,), (320,)).astype(BF16)
    return (layer_out, grad_in, grad_up, grad_up_bias, grad_down.reshape(2560, 320), grad_down_bias)


def solution(mesh):
    return jax.shard_map(
        per_device,
        mesh=mesh,
        in_specs=(
            P(("col", "depth"), "row"),
            P("col", "row"),
            P("row"),
            P("col", "row"),
            P("row"),
            P(("col", "depth"), "row"),
        ),
        out_specs=(
            P(("col", "depth"), "row"),
            P(("col", "depth"), "row"),
            P("col", "row"),
            P("row"),
            P("col", "row"),
            P("row"),
        ),
        check_vma=False,
    )
```

time: 495 us -> 183 us (0.37)
  waiting for transfers between devices: 320 us -> 0 us
  Pallas kernels: 0 us -> 165 us
  blocking collectives: 100 us -> 0 us
  matrix products: 34.7 us -> 0 us
  between operations: 14.2 us -> 0.65 us
  starting transfers between devices: 9.89 us -> 0 us
    pallas_call x0 -> x1, Pallas kernels: none -> 165 us  [per_device(): pl.pallas_call(lambda *refs: kernel(scale, *refs), name='mlp_block', out_...]
    all_gather x4 -> x0, waiting for transfers between devices: 162 us -> none  [the longest x1 75.4 us: per_device(): down_columns = lax.all_gather(down_weight, 'col', axis=0, tiled=True)]
    all_gather x2 -> x0, blocking collectives: 84.3 us -> none  [the longest x1 62.5 us: per_device(): grad_rows = lax.all_gather(out_grad, 'col', axis=0, tiled=True)]
    psum x1 -> x0, waiting for transfers between devices: 74.8 us -> none  [per_device(): lax.psum(up_term.astype(jnp.bfloat16), 'depth').astype(jnp.float32)]
    reduce_scatter x1 -> x0, waiting for transfers between devices: 59 us -> none  [per_device(): lax.psum_scatter(partial_act.astype(jnp.bfloat16), 'row', scatter_dimensi...]
    dot_general x6 -> x0, matrix products: 34.7 us -> none  [the longest x1 7.45 us: per_device(): jnp.dot(full_activ, down_columns, preferred_element_type=jnp.float32)]
    unnamed x8 -> x0, waiting for transfers between devices: 24.4 us -> none
    psum x1 -> x0, blocking collectives: 15.6 us -> none  [per_device(): lax.psum(up_bias_term.astype(jnp.bfloat16), 'depth').astype(jnp.float32)]
  transfers between devices with their start and end apart: 9 -> 0, of which waited for: 6 -> 0; matrix products, arithmetic and copies ran while one was open for 8% -> 0% of each run, Pallas kernels for 0% -> 0%
where the time goes in v1:
time: 183 us; the launch traced here: 180 us
  Pallas kernels  165 us (90%)
  local copies, waits for them, and re-layouts  14.2 us (8%)
    pallas_call x1, Pallas kernels, per_device(): pl.pallas_call(lambda *refs: kernel(scale, *refs), name='mlp_block', out_...  165 us
    unnamed x13, local copies, waits for them, and re-layouts  10.4 us

profile of v1, /device:TPU:1, one launch (start us, length us, event | category | flops | bytes accessed | tf_op | source)
XLA Modules:
  0.0 179.9 jit_solution(1708553089867508005)
XLA Ops:
  0.6 1.3 reshape.29.refs_2_
  1.9 0.0 copy-start.3
  1.9 3.9 %copy.12 = bf16[2560,320]{1,0:T(8,128)(2,1)} copy(bf16[2560,320]{0,1:T(8,128)(2,1)} %param.9) | data formatting | bytes 3276800 | tf_op args[3]
  5.8 0.0 copy-done.3
  5.8 0.6 reshape.31.refs_4_
  6.3 165.1 %mlp_block.1 = (bf16[192,320]{1,0:T(8,128)(2,1)}, bf16[192,320]{1,0:T(8,128)(2,1)}, bf16[640,1280]{1,0:T(8,128)(2,1)}, bf16[4,640,320]{2,1,0:T(8,128)(2,1)}, f32[16,128]{1,0:T(8,128)}, /*index=5*/f32[16,128]{1,0:T(8,128)}) custom-call(bf16[192,320]{1,0:T(8,128)(2,1)} %refs_0_.1, bf16[640,1280]{1,0:T(8,128)(2,1)} %refs_1_.1, f32[1,1280]{1,0:T(1,128)} %reshape.29.refs_2_, ...), custom_call_target="tpu_custom_call" | custom-call | flops 7549747200 | bytes 12582912 | tf_op jit(solution)/shard_map/mlp_block/pallas_call | solution.py:570
  171.4 1.3 slice_bitcast_fusion
  172.7 0.0 copy-start.2
  172.7 0.0 copy-start.1
  172.7 0.0 copy-start
  172.7 4.0 %copy.13 = bf16[2560,320]{0,1:T(8,128)(2,1)} copy(bf16[2560,320]{1,0:T(8,128)(2,1)} %bitcast.6) | data formatting | bytes 3276800
  176.8 0.6 dynamic_slice.5
  177.4 0.0 copy-done.2
  177.4 0.7 copy.17
  178.1 0.0 copy-done.1
  178.1 0.7 copy.18
  178.7 0.0 copy-done
  178.7 1.2 copy.19
Async XLA Ops:
  1.9 3.9 %copy-start.3 = (f32[320]{0:T(512)S(1)}, f32[320]{0:T(512)}, u32[]{:S(2)}) copy-start(f32[320]{0:T(512)} %param.10) | copy-start | bytes 3844
  172.7 4.7 %copy-start.2 = (bf16[192,320]{1,0:T(8,128)(2,1)S(1)}, bf16[192,320]{1,0:T(8,128)(2,1)}, u32[]{:S(2)}) copy-start(bf16[192,320]{1,0:T(8,128)(2,1)} %get-tuple-element.32) | copy-start | bytes 368644
  172.7 5.3 %copy-start.1 = (bf16[192,320]{1,0:T(8,128)(2,1)S(1)}, bf16[192,320]{1,0:T(8,128)(2,1)}, u32[]{:S(2)}) copy-start(bf16[192,320]{1,0:T(8,128)(2,1)} %get-tuple-element.33) | copy-start | bytes 368644
  172.7 6.0 %copy-start = (bf16[640,1280]{1,0:T(8,128)(2,1)S(1)}, bf16[640,1280]{1,0:T(8,128)(2,1)}, u32[]{:S(2)}) copy-start(bf16[640,1280]{1,0:T(8,128)(2,1)} %get-tuple-element.34) | copy-start | bytes 4915204

commit v2 on v1

v2 whole, which is shorter than its diff:
```python
import math

import jax
import jax.numpy as jnp
from jax import lax
from jax.experimental import pallas as pl
from jax.experimental.pallas import tpu as pltpu
from jax.sharding import PartitionSpec as P

GELU_C = math.sqrt(2.0 / math.pi)
MESH = pl.DeviceIdType.MESH
F32 = jnp.float32
BF16 = jnp.bfloat16
N_SEMS = 320


def gelu_parts(v):
    t = jnp.tanh(GELU_C * (v + 0.044715 * v * v * v))
    value = 0.5 * v * (1.0 + t)
    slope = 0.5 * (1.0 + t) + 0.5 * v * (1.0 - t * t) * GELU_C * (1.0 + 3.0 * 0.044715 * v * v)
    return value, slope


def nn(a, b):
    return lax.dot_general(a, b, (((1,), (0,)), ((), ())), preferred_element_type=F32)


def nt(a, b):
    return lax.dot_general(a, b, (((1,), (1,)), ((), ())), preferred_element_type=F32)


def rows(start, size, tile=16):
    return pl.ds(pl.multiple_of(start, tile), size)


def kernel(
    scale,
    tok, wu_in, bu_in, wd_in, bd_in, grad,
    o_out, gi_out, gu_out, gd_out, bu_out, bd_out,
    xr, piece, bb, bbr,
    full, wts, full_t,
    hps, hpr, hpo, slope, act, dhid,
    part, ra, rb, xsum, zr, osend, orecv,
    gpart, ga, gb, gz, gfin,
    bt, br, yb, pb,
    sems,
):
    row, y, dep = lax.axis_index("row"), lax.axis_index("col"), lax.axis_index("depth")
    h, k = row // 2, lax.rem(row, 2)
    zl, x = dep // 4, lax.rem(dep, 4)
    hh = h // 2
    hi = lax.rem(h, 2)

    def at(h_, k_, y_):
        return (h_ * 2 + k_, y_, dep)

    def dep_at(a, b):
        return (row, y, lax.rem(zl + b, 2) * 4 + lax.rem(x + a, 4))

    def y_at(a):
        return (row, lax.rem(y + a, 4), dep)

    partner = (h * 2 + 1 - k, y, dep)
    zpeer = dep_at(0, 1)

    bar = pltpu.get_barrier_semaphore()
    fixed = [partner] + [y_at(a) for a in (1, 2, 3)]
    fixed += [dep_at(a, b) for a in range(4) for b in range(2) if (a, b) != (0, 0)]
    for target in fixed:
        pl.semaphore_signal(bar, inc=1, device_id=target, device_id_type=MESH)
    count = len(fixed)

    def greet(h_, k_, y_):
        other = jnp.logical_not((h_ == h) & (k_ == k) & (y_ == y))

        @pl.when(other)
        def _():
            pl.semaphore_signal(bar, inc=1, device_id=at(h_, k_, y_), device_id_type=MESH)

        return other.astype(jnp.int32)

    for a in range(4):
        count = count + greet(a, hh, y)
        count = count + greet(y, hh, a)
    for a in range(2):
        for b in range(2):
            count = count + greet(2 * k + a, b, y)
            count = count + greet(2 * k + a, b, h)
        count = count + greet(h, y // 2, 2 * k + a)
    pl.semaphore_wait(bar, count)

    used = [0]
    sent = []

    def new(n=1):
        first = used[0]
        used[0] += n
        return first

    def send(src, dst, rsem, target):
        copy = pltpu.make_async_remote_copy(
            src_ref=src, dst_ref=dst, send_sem=sems.at[new()], recv_sem=sems.at[rsem],
            device_id=target, device_id_type=MESH,
        )
        copy.start()
        sent.append((copy, None))

    def send_maybe(src, dst, rsem, h_, k_, y_):
        mine = (h_ == h) & (k_ == k) & (y_ == y)
        copy = pltpu.make_async_remote_copy(
            src_ref=src, dst_ref=dst, send_sem=sems.at[new()], recv_sem=sems.at[rsem],
            device_id=at(h_, k_, y_), device_id_type=MESH,
        )

        @pl.when(jnp.logical_not(mine))
        def _():
            copy.start()

        @pl.when(mine)
        def _():
            pltpu.make_async_copy(src, dst, sems.at[rsem]).start()

        sent.append((copy, jnp.logical_not(mine)))

    def got(dst, rsem):
        pltpu.make_async_copy(dst, dst, sems.at[rsem]).wait()

    def chunk(buf):
        return lambda i, q: buf.at[i, :, rows(lax.rem(q, 4) * 80, 80)]

    def token_rows(buf):
        return lambda i, q: buf.at[i, rows(lax.rem(q, 4) * 192, 192)]

    def ring(axis):
        if axis == "y":
            return y, y_at(1), y_at(3)
        return x, dep_at(1, 0), dep_at(3, 0)

    class Gather:
        def __init__(self, view, axis):
            self.p, self.right, self.left = ring(axis)
            self.view = view
            self.s_right, self.s_left, self.s_fwd = new(2), new(2), new(2)

        def first(self, i):
            mine = self.view(i, self.p)
            pair = [(self.s_right + i, self.right), (self.s_left + i, self.left)]
            for sem, target in pair if i == 0 else pair[::-1]:
                send(mine, mine, sem, target)

        def forward(self, i):
            if i == 0:
                block = self.view(0, self.p + 3)
                got(block, self.s_right)
                send(block, block, self.s_fwd, self.right)
            else:
                block = self.view(1, self.p + 1)
                got(block, self.s_left + 1)
                send(block, block, self.s_fwd + 1, self.left)

        def finish(self):
            got(self.view(1, self.p + 3), self.s_right + 1)
            got(self.view(0, self.p + 1), self.s_left)
            got(self.view(0, self.p + 2), self.s_fwd)
            got(self.view(1, self.p + 2), self.s_fwd + 1)

    class Reduce:
        def __init__(self, view, first, second, axis):
            self.p, self.right, self.left = ring(axis)
            self.view = view
            self.first, self.second = first, second
            self.s1, self.s2 = new(2), new(4)

        def far(self):
            send(self.view(0, self.p + 2), self.first.at[0], self.s1, self.right)
            send(self.view(1, self.p + 2), self.first.at[1], self.s1 + 1, self.left)

        def near(self):
            send(self.view(1, self.p + 1), self.second.at[0, 1], self.s2 + 1, self.right)
            send(self.view(0, self.p + 3), self.second.at[1, 0], self.s2 + 2, self.left)

        def middle(self):
            for i, q, target in ((0, self.p + 1, self.right), (1, self.p + 3, self.left)):
                got(self.first.at[i], self.s1 + i)
                block = self.view(i, q)
                block[...] = (block[...].astype(F32) + self.first[i].astype(F32)).astype(BF16)
                send(block, self.second.at[i, i], self.s2 + 3 * i, target)

        def total(self, i):
            got(self.second.at[0, i], self.s2 + i)
            got(self.second.at[1, i], self.s2 + 2 + i)
            return (
                self.view(i, self.p)[...].astype(F32)
                + self.second[0, i].astype(F32)
                + self.second[1, i].astype(F32)
            )

    def pair_lanes(own, other):
        first = jnp.where(k == 0, own, other).astype(F32)
        second = jnp.where(k == 0, other, own).astype(F32)
        return jnp.concatenate([first, second], axis=1).astype(BF16)

    def split_lanes(both):
        low, high = both[:, :320], both[:, 320:]
        return jnp.where(k == 0, low, high), jnp.where(k == 0, high, low)

    s_x = new(2)
    for n, src in enumerate((tok, grad)):
        send(src.at[rows((1 - k) * 96, 96)], xr.at[n], s_x + n, partner)
    quarter = rows(x * 80, 80)
    s_w = [new(2), new(4)]
    for j in range(2):
        send_maybe(
            wu_in.at[:, quarter, pl.ds(j * 640, 640)],
            wts.at[0, lax.rem(y, 2), :, quarter],
            s_w[0] + lax.rem(y, 2), h, y // 2, 2 * k + j,
        )
    bb[...] = jnp.broadcast_to(bu_in[...], bb.shape)
    s_bb = new(1)
    send(bb, bbr, s_bb, partner)

    s_piece = [new(4), new(4)]

    def send_piece(n, src):
        got(xr.at[n], s_x + n)
        piece[n] = pair_lanes(src[rows(k * 96, 96), :], xr[n])
        for a in range(4):
            send_maybe(
                piece.at[n],
                full.at[n, hi, rows(y * 192 + k * 96, 96)],
                s_piece[n] + hi * 2 + k, lax.rem(h + a, 4), hh, y,
            )

    def got_pieces(n, i):
        for kk in range(2):
            got(full.at[n, i, rows(y * 192 + kk * 96, 96)], s_piece[n] + i * 2 + kk)

    send_piece(0, tok)
    for j in range(4):
        send_maybe(
            wd_in.at[quarter, pl.ds(j * 640, 640)],
            wts.at[1, hi, k, quarter],
            s_w[1] + hi * 2 + k, y, hh, j,
        )
    send_piece(1, grad)

    wag = [Gather(chunk(wts.at[n]), "x") for n in range(2)]
    tag = [Gather(token_rows(full.at[n]), "y") for n in range(2)]

    for i in range(2):
        got(wts.at[0, i, :, quarter], s_w[0] + i)
        wag[0].first(i)
    for i in range(2):
        got_pieces(0, i)
        tag[0].first(i)
    for i in range(2):
        wag[0].forward(i)
    for i in range(2):
        tag[0].forward(i)
    for i in range(2):
        for kk in range(2):
            got(wts.at[1, i, kk, quarter], s_w[1] + i * 2 + kk)
        wag[1].first(i)
    for i in range(2):
        got_pieces(1, i)
        tag[1].first(i)

    half = 384
    own_rows = rows(k * half, half)
    other_rows = rows((1 - k) * half, half)

    def weight(n, i):
        return wts[n, i].reshape(640, 640)

    def hidden(n, block):
        return nn(full[n, 0, block], weight(n, 0)) + nn(full[n, 1, block], weight(n, 1))

    def transpose(n):
        for i in range(2):
            full_t[n, i] = full[n, i].T.reshape(2, 320, 768)

    s_hp, s_act = [new(1), new(1)], [new(1), new(1)]
    tag[0].finish()
    wag[0].finish()
    hps[0] = hidden(0, other_rows)
    send(hps.at[0], hpr.at[0], s_hp[0], partner)
    hpo[...] = hidden(0, own_rows)
    for i in range(2):
        wag[1].forward(i)
    for i in range(2):
        tag[1].forward(i)
    transpose(0)
    got(bbr, s_bb)
    low = jnp.where(k == y // 2, bb[0:1], bbr[0:1])
    bias = jnp.where(lax.rem(y, 2) == 0, low[:, :640], low[:, 640:])
    got(hpr.at[0], s_hp[0])
    value, slope_now = gelu_parts(hpo[...] + hpr[0] + bias)
    slope[...] = slope_now
    act[own_rows] = value.astype(BF16)
    send(act.at[own_rows], act.at[own_rows], s_act[0], partner)

    tag[1].finish()
    transpose(1)
    wag[1].finish()
    hps[1] = hidden(1, other_rows)
    send(hps.at[1], hpr.at[1], s_hp[1], partner)
    got(act.at[other_rows], s_act[0])

    ored = [Reduce(token_rows(part.at[n]), ra.at[n], rb.at[n], "y") for n in range(2)]
    gred = [Reduce(chunk(gpart.at[n]), ga.at[n], gb.at[n], "x") for n in range(2)]

    def out_block(n, q):
        block = rows(lax.rem(q, 4) * 192, 192)
        left = act if n == 0 else dhid
        for i in range(2):
            part[n, i, block] = nt(left[block], weight(1 - n, i)).astype(BF16)

    def grad_block(n, q):
        block = rows(lax.rem(q, 4) * 80, 80)
        right = dhid if n == 0 else act
        for i in range(2):
            left = full_t[n, i, :, block].reshape(160, 768)
            gpart[n, i, :, block] = (nn(left, right[...]) * scale).astype(BF16).reshape(2, 80, 640)

    grad_block(1, x + 2)
    gred[1].far()
    out_block(0, y + 2)
    ored[0].far()
    grad_block(1, x + 1)
    grad_block(1, x + 3)
    gred[1].near()
    out_block(0, y + 1)
    out_block(0, y + 3)
    ored[0].near()
    d_own = hidden(1, own_rows)
    got(hpr.at[1], s_hp[1])
    dhid[own_rows] = ((d_own + hpr[1]) * slope[...]).astype(BF16)
    send(dhid.at[own_rows], dhid.at[own_rows], s_act[1], partner)
    grad_block(1, x)
    gred[1].middle()
    got(dhid.at[other_rows], s_act[1])
    grad_block(0, x + 2)
    gred[0].far()
    ored[0].middle()
    out_block(1, y + 2)
    ored[1].far()
    grad_block(0, x + 1)
    grad_block(0, x + 3)
    gred[0].near()
    out_block(1, y + 1)
    out_block(1, y + 3)
    ored[1].near()
    grad_block(0, x)
    out_block(0, y)
    out_block(1, y)

    ones = jnp.ones((16, 768), BF16)
    terms = [nn(ones, dhid[...]), nn(ones, full[1, 0]), nn(ones, full[1, 1])]
    bt[...] = jnp.zeros_like(bt)
    for n in range(15):
        term = terms[n // 5][0:1, (n % 5) * 128 : (n % 5 + 1) * 128] * scale
        bt[n : n + 1] = term.astype(BF16).astype(F32)
    br[dep] = bt[...]
    s_bt = new(8)
    for a in range(4):
        for b in range(2):
            if (a, b) != (0, 0):
                send(bt, br.at[dep], s_bt + a * 2 + b, dep_at(a, b))

    s_oz = [new(4), new(4)]

    def out_z(n):
        for i in range(2):
            xsum[n, i] = ored[n].total(i).astype(BF16)
            for kk in range(2):
                send_maybe(
                    xsum.at[n, i, pl.ds(kk * 96, 96)], zr.at[n, h], s_oz[n] + h, 2 * k + i, kk, y
                )

    s_gz, s_gr = [new(2), new(2)], [new(2), new(4)]

    def grad_zl(n):
        for i in range(2):
            gz[n, 0, i] = gred[n].total(i).astype(BF16)
            send(gz.at[n, 0, i], gz.at[n, 1, i], s_gz[n] + i, zpeer)

    def grad_home(n):
        for i in range(2):
            got(gz.at[n, 1, i], s_gz[n] + i)
            gfin[n, i] = (gz[n, 0, i].astype(F32) + gz[n, 1, i].astype(F32)).astype(BF16)
            if n == 0:
                lanes = pl.ds(pl.multiple_of(lax.rem(y, 2) * 640, 128), 640)
                send_maybe(
                    gfin.at[0, i], gu_out.at[:, quarter, lanes],
                    s_gr[0] + lax.rem(y, 2), h, y // 2, 2 * k + i,
                )
            else:
                lanes = pl.ds(pl.multiple_of(y * 640, 128), 640)
                for kk in range(2):
                    send_maybe(
                        gfin.at[1, i, kk], gd_out.at[quarter, lanes], s_gr[1] + y, 2 * k + i, kk, h
                    )

    back = [
        Gather(lambda i, q: gu_out.at[:, rows(lax.rem(q, 4) * 80, 80), pl.ds(i * 640, 640)], "x"),
        Gather(lambda i, q: gd_out.at[rows(lax.rem(q, 4) * 80, 80), pl.ds(i * 1280, 1280)], "x"),
    ]

    def back_first(n):
        for i in range(2):
            if n == 0:
                got(gu_out.at[:, quarter, pl.ds(i * 640, 640)], s_gr[0] + i)
            else:
                for j in range(2):
                    got(gd_out.at[quarter, pl.ds((2 * i + j) * 640, 640)], s_gr[1] + 2 * i + j)
            back[n].first(i)

    s_of = [new(1), new(1)]

    def out_last(n):
        total = jnp.zeros((96, 640), F32)
        for a in range(4):
            got(zr.at[n, a], s_oz[n] + a)
            total = total + zr[n, a].astype(F32)
        mine, theirs = split_lanes(total)
        osend[n] = theirs
        send(osend.at[n], orecv.at[n], s_of[n], partner)
        if n == 0:
            o_out[rows(k * 96, 96)] = (mine + bd_in[...]).astype(BF16)
        else:
            gi_out[rows(k * 96, 96)] = mine.astype(BF16)

    grad_zl(1)
    gred[0].middle()
    ored[1].middle()
    grad_home(1)
    out_z(0)
    grad_zl(0)
    back_first(1)
    out_z(1)
    grad_home(0)

    for a in range(4):
        for b in range(2):
            if (a, b) != (0, 0):
                from_dep = lax.rem(zl + b, 2) * 4 + lax.rem(x + 4 - a, 4)
                got(br.at[from_dep], s_bt + a * 2 + b)
    total = br[0]
    for n in range(1, 8):
        total = total + br[n]
    yb[y] = total
    s_yb = new(4)
    for a in range(1, 4):
        send(yb.at[y], yb.at[y], s_yb + a, y_at(a))
    s_pb = new(1)
    send(yb.at[y], pb, s_pb, partner)

    for i in range(2):
        back[1].forward(i)
    back_first(0)
    out_last(0)
    for i in range(2):
        back[0].forward(i)
    out_last(1)
    got(orecv.at[0], s_of[0])
    o_out[rows((1 - k) * 96, 96)] = (orecv[0] + bd_in[...]).astype(BF16)
    for a in range(1, 4):
        got(yb.at[lax.rem(y + 4 - a, 4)], s_yb + a)
    got(pb, s_pb)
    bu_out[0:5] = yb[2 * k][0:5]
    bu_out[5:10] = yb[2 * k + 1][0:5]
    bd_out[0:10] = jnp.where(k == hh, yb[y][5:15], pb[5:15])
    got(orecv.at[1], s_of[1])
    gi_out[rows((1 - k) * 96, 96)] = orecv[1].astype(BF16)
    back[1].finish()
    back[0].finish()

    for copy, when in sent:
        if when is None:
            copy.wait_send()
        else:

            @pl.when(when)
            def _(copy=copy):
                copy.wait_send()

    assert used[0] <= N_SEMS, used[0]


def per_device(tokens, up_weight, up_bias, down_weight, down_bias, out_grad):
    token_rows = tokens.shape[0]
    scale = 1.0 / math.sqrt(token_rows * lax.axis_size("col") * lax.axis_size("depth"))
    vmem = pl.BlockSpec(memory_space=pltpu.VMEM)
    hbm = pl.BlockSpec(memory_space=pl.ANY)
    scratch = [
        ((2, 96, 320), BF16),
        ((2, 96, 640), BF16),
        ((8, 1280), F32),
        ((8, 1280), F32),
        ((2, 2, 768, 640), BF16),
        ((2, 2, 2, 320, 640), BF16),
        ((2, 2, 2, 320, 768), BF16),
        ((2, 384, 640), F32),
        ((2, 384, 640), F32),
        ((384, 640), F32),
        ((384, 640), F32),
        ((768, 640), BF16),
        ((768, 640), BF16),
        ((2, 2, 768, 640), BF16),
        ((2, 2, 192, 640), BF16),
        ((2, 2, 2, 192, 640), BF16),
        ((2, 2, 192, 640), BF16),
        ((2, 4, 96, 640), BF16),
        ((2, 96, 320), F32),
        ((2, 96, 320), F32),
        ((2, 2, 2, 320, 640), BF16),
        ((2, 2, 2, 80, 640), BF16),
        ((2, 2, 2, 2, 80, 640), BF16),
        ((2, 2, 2, 2, 80, 640), BF16),
        ((2, 2, 2, 80, 640), BF16),
        ((16, 128), F32),
        ((8, 16, 128), F32),
        ((4, 16, 128), F32),
        ((16, 128), F32),
    ]
    out = pl.pallas_call(
        lambda *refs: kernel(scale, *refs),
        name="mlp_block",
        out_shape=[
            jax.ShapeDtypeStruct((192, 320), BF16),
            jax.ShapeDtypeStruct((192, 320), BF16),
            jax.ShapeDtypeStruct((2, 320, 1280), BF16),
            jax.ShapeDtypeStruct((320, 2560), BF16),
            jax.ShapeDtypeStruct((16, 128), F32),
            jax.ShapeDtypeStruct((16, 128), F32),
        ],
        in_specs=[vmem, hbm, vmem, hbm, vmem, vmem],
        out_specs=[vmem] * 6,
        scratch_shapes=[pltpu.VMEM(*s) for s in scratch] + [pltpu.SemaphoreType.DMA((N_SEMS,))],
        compiler_params=pltpu.CompilerParams(
            collective_id=0, has_side_effects=True, vmem_limit_bytes=56 << 20
        ),
        cost_estimate=pl.CostEstimate(
            flops=6 * 2 * 768 * 1280 * 640, bytes_accessed=12 << 20, transcendentals=384 * 640
        ),
    )(
        tokens,
        up_weight.reshape(2, 320, 1280),
        up_bias.reshape(1, 1280),
        down_weight.T,
        down_bias.reshape(1, 320),
        out_grad,
    )
    layer_out, grad_in, grad_up, grad_down, bu, bd = out
    row = lax.axis_index("row")
    grad_up_bias = bu[:10].reshape(1280).astype(BF16)
    start = lax.rem(row // 2, 2) * 640 + lax.rem(row, 2) * 320
    grad_down_bias = lax.dynamic_slice(bd[:10].reshape(1280), (start,), (320,)).astype(BF16)
    grad_up = grad_up.reshape(640, 1280)
    return (layer_out, grad_in, grad_up, grad_up_bias, grad_down.T, grad_down_bias)


def solution(mesh):
    return jax.shard_map(
        per_device,
        mesh=mesh,
        in_specs=(
            P(("col", "depth"), "row"),
            P("col", "row"),
            P("row"),
            P("col", "row"),
            P("row"),
            P(("col", "depth"), "row"),
        ),
        out_specs=(
            P(("col", "depth"), "row"),
            P(("col", "depth"), "row"),
            P("col", "row"),
            P("row"),
            P("col", "row"),
            P("row"),
        ),
        check_vma=False,
    )
```

time: 183 us -> 171 us (0.934)
  the two profiles are of different devices: /device:TPU:1 before, /device:TPU:88 now
where the time goes in v2:
time: 171 us
  Pallas kernels  158 us (92%)
  local copies, waits for them, and re-layouts  11.6 us (7%)
    pallas_call x1, Pallas kernels, per_device(): pl.pallas_call(lambda *refs: kernel(scale, *refs), name='mlp_block', out_...  158 us
    unnamed x6, local copies, waits for them, and re-layouts  7.16 us

profile of v2, /device:TPU:88, one launch (start us, length us, event | category | flops | bytes accessed | tf_op | source)
XLA Modules:
  0.0 170.5 jit_solution(3589143487853136456)
XLA Ops:
  0.7 1.2 reshape.31.refs_4_
  1.9 1.3 reshape.30.refs_2_
  3.2 158.2 %mlp_block.1 = (bf16[192,320]{1,0:T(8,128)(2,1)}, bf16[192,320]{1,0:T(8,128)(2,1)}, bf16[2,320,1280]{2,1,0:T(8,128)(2,1)}, bf16[320,2560]{1,0:T(8,128)(2,1)}, f32[16,128]{1,0:T(8,128)}, /*index=5*/f32[16,128]{1,0:T(8,128)}) custom-call(bf16[192,320]{1,0:T(8,128)(2,1)} %refs_0_.1, bf16[2,320,1280]{2,1,0:T(8,128)(2,1)} %bitcast.10, ...), custom_call_target="tpu_custom_call" | custom-call | flops 7549747200 | bytes 12582912 | tf_op jit(solution)/shard_map/mlp_block/pallas_call | solution.py:526
  161.4 1.3 slice_bitcast_fusion
  162.7 0.6 dynamic_slice.5
  163.4 1.6 copy.16
  164.9 1.6 copy.17
  166.5 0.0 copy-start
  166.5 2.8 %copy.18 = bf16[640,1280]{1,0:T(8,128)(2,1)} copy(bf16[640,1280]{1,0:T(8,128)(2,1)} %bitcast.9) | data formatting | bytes 3276800
  169.4 0.0 copy-done
  169.4 1.2 copy.19
Async XLA Ops:
  166.5 2.8 %copy-start = (bf16[320,2560]{1,0:T(8,128)(2,1)S(1)}, bf16[320,2560]{1,0:T(8,128)(2,1)}, u32[]{:S(2)}) copy-start(bf16[320,2560]{1,0:T(8,128)(2,1)} %get-tuple-element.16) | copy-start | bytes 4915204

commit v3 on v2

--- a/solution.py
+++ b/solution.py
@@ -37,11 +37,11 @@
     scale,
     tok, wu_in, bu_in, wd_in, bd_in, grad,
     o_out, gi_out, gu_out, gd_out, bu_out, bd_out,
-    xr, piece, bb, bbr,
+    xr, piece, wq, bb, bbr,
     full, wts, full_t,
     hps, hpr, hpo, slope, act, dhid,
     part, ra, rb, xsum, zr, osend, orecv,
-    gpart, ga, gb, gz, gfin,
+    gpart, ga, gb, gsum, gs, gz, gfin,
     bt, br, yb, pb,
     sems,
 ):
@@ -51,8 +51,14 @@
     hh = h // 2
     hi = lax.rem(h, 2)
 
-    def at(h_, k_, y_):
-        return (h_ * 2 + k_, y_, dep)
+    def at(h_, k_, y_, plane):
+        return (h_ * 2 + k_, y_, plane * 4 + x)
+
+    def is_me(h_, k_, y_, plane):
+        return (h_ == h) & (k_ == k) & (y_ == y) & (plane == zl)
+
+    def z_at(a):
+        return (lax.rem(h + a, 4) * 2 + k, y, dep)
 
     def dep_at(a, b):
         return (row, y, lax.rem(zl + b, 2) * 4 + lax.rem(x + a, 4))
@@ -64,29 +70,29 @@
     zpeer = dep_at(0, 1)
 
     bar = pltpu.get_barrier_semaphore()
-    fixed = [partner] + [y_at(a) for a in (1, 2, 3)]
+    fixed = [partner, z_at(1), z_at(3)] + [y_at(a) for a in (1, 2, 3)]
     fixed += [dep_at(a, b) for a in range(4) for b in range(2) if (a, b) != (0, 0)]
     for target in fixed:
         pl.semaphore_signal(bar, inc=1, device_id=target, device_id_type=MESH)
     count = len(fixed)
 
-    def greet(h_, k_, y_):
-        other = jnp.logical_not((h_ == h) & (k_ == k) & (y_ == y))
+    def greet(*place):
+        other = jnp.logical_not(is_me(*place))
 
         @pl.when(other)
         def _():
-            pl.semaphore_signal(bar, inc=1, device_id=at(h_, k_, y_), device_id_type=MESH)
+            pl.semaphore_signal(bar, inc=1, device_id=at(*place), device_id_type=MESH)
 
         return other.astype(jnp.int32)
 
     for a in range(4):
-        count = count + greet(a, hh, y)
-        count = count + greet(y, hh, a)
+        count = count + greet(a, hh, y, zl)
+        count = count + greet(y, hh, a, k)
     for a in range(2):
         for b in range(2):
-            count = count + greet(2 * k + a, b, y)
-            count = count + greet(2 * k + a, b, h)
-        count = count + greet(h, y // 2, 2 * k + a)
+            count = count + greet(2 * k + a, b, y, zl)
+            count = count + greet(2 * k + a, zl, h, b)
+            count = count + greet(h, y // 2, 2 * k + a, b)
     pl.semaphore_wait(bar, count)
 
     used = [0]
@@ -105,31 +111,43 @@
         copy.start()
         sent.append((copy, None))
 
-    def send_maybe(src, dst, rsem, h_, k_, y_):
-        mine = (h_ == h) & (k_ == k) & (y_ == y)
+    def send_if(only, src, dst, rsem, *place):
+        mine = is_me(*place)
+        away = jnp.logical_not(mine) & only
         copy = pltpu.make_async_remote_copy(
             src_ref=src, dst_ref=dst, send_sem=sems.at[new()], recv_sem=sems.at[rsem],
-            device_id=at(h_, k_, y_), device_id_type=MESH,
+            device_id=at(*place), device_id_type=MESH,
         )
 
-        @pl.when(jnp.logical_not(mine))
+        @pl.when(away)
         def _():
             copy.start()
 
-        @pl.when(mine)
+        @pl.when(mine & only)
         def _():
             pltpu.make_async_copy(src, dst, sems.at[rsem]).start()
 
-        sent.append((copy, jnp.logical_not(mine)))
+        sent.append((copy, away))
 
     def got(dst, rsem):
         pltpu.make_async_copy(dst, dst, sems.at[rsem]).wait()
 
-    def chunk(buf):
+    def got_if(only, dst, rsem):
+        @pl.when(only)
+        def _():
+            got(dst, rsem)
+
+    def token_view(buf):
+        return lambda i, q: buf.at[i, rows(lax.rem(q, 4) * 192, 192)]
+
+    def half_view(buf, i):
+        return lambda kk, q: buf.at[i, rows(lax.rem(q, 4) * 192 + kk * 96, 96)]
+
+    def chunk_view(buf):
         return lambda i, q: buf.at[i, :, rows(lax.rem(q, 4) * 80, 80)]
 
-    def token_rows(buf):
-        return lambda i, q: buf.at[i, rows(lax.rem(q, 4) * 192, 192)]
+    def chunk_half_view(buf, i):
+        return lambda kk, q: buf.at[i, kk, rows(lax.rem(q, 4) * 80, 80)]
 
     def ring(axis):
         if axis == "y":
@@ -208,62 +226,90 @@
     for n, src in enumerate((tok, grad)):
         send(src.at[rows((1 - k) * 96, 96)], xr.at[n], s_x + n, partner)
     quarter = rows(x * 80, 80)
+    always = k >= 0
+
+    def lanes(n):
+        return pl.ds(pl.multiple_of(n * 640, 128), 640)
+
     s_w = [new(2), new(4)]
     for j in range(2):
-        send_maybe(
+        send_if(
+            always,
             wu_in.at[:, quarter, pl.ds(j * 640, 640)],
             wts.at[0, lax.rem(y, 2), :, quarter],
-            s_w[0] + lax.rem(y, 2), h, y // 2, 2 * k + j,
+            s_w[0] + lax.rem(y, 2), h, y // 2, 2 * k + j, zl,
         )
+    s_wq = new(4)
+    for a in range(4):
+        y_to = lax.rem(y + a, 4)
+        send_if(always, wd_in.at[quarter, lanes(y_to)], wq.at[y], s_wq + a, h, k, y_to, zl)
     bb[...] = jnp.broadcast_to(bu_in[...], bb.shape)
     s_bb = new(1)
     send(bb, bbr, s_bb, partner)
 
     s_piece = [new(4), new(4)]
+    to_right = [h == lax.rem(2 * k + i + 1, 4) for i in range(2)]
+    to_left = [h == lax.rem(2 * k + i + 3, 4) for i in range(2)]
+
+    def part_of(n, i, kk):
+        return full.at[n, i, rows(y * 192 + kk * 96, 96)]
 
     def send_piece(n, src):
         got(xr.at[n], s_x + n)
         piece[n] = pair_lanes(src[rows(k * 96, 96), :], xr[n])
-        for a in range(4):
-            send_maybe(
-                piece.at[n],
-                full.at[n, hi, rows(y * 192 + k * 96, 96)],
-                s_piece[n] + hi * 2 + k, lax.rem(h + a, 4), hh, y,
-            )
-
-    def got_pieces(n, i):
-        for kk in range(2):
-            got(full.at[n, i, rows(y * 192 + kk * 96, 96)], s_piece[n] + i * 2 + kk)
+        dst = part_of(n, hi, k)
+        sem = s_piece[n] + hi * 2 + k
+        for a in (1, 3):
+            send_if(always, piece.at[n], dst, sem, lax.rem(h + a, 4), hh, y, zl)
+        send_if(always, piece.at[n], dst, sem, h, hh, y, zl)
+
+    def pass_piece(n):
+        for i in range(2):
+            for kk, only, a in ((0, to_right[i], 1), (1, to_left[i], 3)):
+                sem = s_piece[n] + i * 2 + kk
+                block = part_of(n, i, kk)
+                got_if(only, block, sem)
+                send_if(only, block, block, sem, lax.rem(h + a, 4), k, y, zl)
+
+    def got_piece(n, i, kk):
+        only = (to_right, to_left)[kk][i]
+        got_if(jnp.logical_not(only), part_of(n, i, kk), s_piece[n] + i * 2 + kk)
+
+    wag = [Gather(chunk_view(wts.at[n]), "x") for n in range(2)]
+    tag = [[Gather(half_view(full.at[n], i), "y") for i in range(2)] for n in range(2)]
+
+    def over_y(n, i, kk):
+        got_piece(n, i, kk)
+        tag[n][i].first(kk)
 
     send_piece(0, tok)
-    for j in range(4):
-        send_maybe(
-            wd_in.at[quarter, pl.ds(j * 640, 640)],
-            wts.at[1, hi, k, quarter],
-            s_w[1] + hi * 2 + k, y, hh, j,
-        )
-    send_piece(1, grad)
-
-    wag = [Gather(chunk(wts.at[n]), "x") for n in range(2)]
-    tag = [Gather(token_rows(full.at[n]), "y") for n in range(2)]
-
     for i in range(2):
         got(wts.at[0, i, :, quarter], s_w[0] + i)
         wag[0].first(i)
-    for i in range(2):
-        got_pieces(0, i)
-        tag[0].first(i)
+    pass_piece(0)
+    for a in range(4):
+        origin = lax.rem(y + 4 - a, 4)
+        got(wq.at[origin], s_wq + a)
+        send_if(
+            always, wq.at[origin], wts.at[1, hi, k, quarter], s_w[1] + hi * 2 + k, origin, hh, y, zl
+        )
+    for i in range(2):
+        for kk in range(2):
+            over_y(0, i, kk)
+    send_piece(1, grad)
     for i in range(2):
         wag[0].forward(i)
     for i in range(2):
-        tag[0].forward(i)
+        for kk in range(2):
+            tag[0][i].forward(kk)
     for i in range(2):
         for kk in range(2):
             got(wts.at[1, i, kk, quarter], s_w[1] + i * 2 + kk)
         wag[1].first(i)
-    for i in range(2):
-        got_pieces(1, i)
-        tag[1].first(i)
+    pass_piece(1)
+    over_y(1, 0, 0)
+    over_y(1, 0, 1)
+    over_y(1, 1, 0)
 
     half = 384
     own_rows = rows(k * half, half)
@@ -275,21 +321,19 @@
     def hidden(n, block):
         return nn(full[n, 0, block], weight(n, 0)) + nn(full[n, 1, block], weight(n, 1))
 
-    def transpose(n):
-        for i in range(2):
-            full_t[n, i] = full[n, i].T.reshape(2, 320, 768)
+    def transpose(n, i):
+        full_t[n, i] = full[n, i].T.reshape(2, 320, 768)
 
     s_hp, s_act = [new(1), new(1)], [new(1), new(1)]
-    tag[0].finish()
+    tag[0][0].finish()
+    tag[0][1].finish()
     wag[0].finish()
     hps[0] = hidden(0, other_rows)
     send(hps.at[0], hpr.at[0], s_hp[0], partner)
     hpo[...] = hidden(0, own_rows)
-    for i in range(2):
-        wag[1].forward(i)
-    for i in range(2):
-        tag[1].forward(i)
-    transpose(0)
+    for kk in range(2):
+        tag[1][0].forward(kk)
+    over_y(1, 1, 1)
     got(bbr, s_bb)
     low = jnp.where(k == y // 2, bb[0:1], bbr[0:1])
     bias = jnp.where(lax.rem(y, 2) == 0, low[:, :640], low[:, 640:])
@@ -298,16 +342,17 @@
     slope[...] = slope_now
     act[own_rows] = value.astype(BF16)
     send(act.at[own_rows], act.at[own_rows], s_act[0], partner)
-
-    tag[1].finish()
-    transpose(1)
-    wag[1].finish()
-    hps[1] = hidden(1, other_rows)
-    send(hps.at[1], hpr.at[1], s_hp[1], partner)
+    for i in range(2):
+        transpose(0, i)
+    for i in range(2):
+        wag[1].forward(i)
     got(act.at[other_rows], s_act[0])
 
-    ored = [Reduce(token_rows(part.at[n]), ra.at[n], rb.at[n], "y") for n in range(2)]
-    gred = [Reduce(chunk(gpart.at[n]), ga.at[n], gb.at[n], "x") for n in range(2)]
+    ored = [Reduce(token_view(part.at[n]), ra.at[n], rb.at[n], "y") for n in range(2)]
+    gred = [
+        [Reduce(chunk_half_view(gpart.at[n], i), ga.at[n, i], gb.at[n, i], "x") for i in range(2)]
+        for n in range(2)
+    ]
 
     def out_block(n, q):
         block = rows(lax.rem(q, 4) * 192, 192)
@@ -315,45 +360,131 @@
         for i in range(2):
             part[n, i, block] = nt(left[block], weight(1 - n, i)).astype(BF16)
 
-    def grad_block(n, q):
+    def grad_block(n, i, q):
         block = rows(lax.rem(q, 4) * 80, 80)
         right = dhid if n == 0 else act
+        left = full_t[n, i, :, block].reshape(160, 768)
+        gpart[n, i, :, block] = (nn(left, right[...]) * scale).astype(BF16).reshape(2, 80, 640)
+
+    def grad_start(n, i):
+        grad_block(n, i, x + 2)
+        gred[n][i].far()
+        grad_block(n, i, x + 1)
+        grad_block(n, i, x + 3)
+        gred[n][i].near()
+
+    def grad_middle(n, i):
+        grad_block(n, i, x)
+        gred[n][i].middle()
+
+    s_oz = [new(4), new(4)]
+
+    def out_z(n):
         for i in range(2):
-            left = full_t[n, i, :, block].reshape(160, 768)
-            gpart[n, i, :, block] = (nn(left, right[...]) * scale).astype(BF16).reshape(2, 80, 640)
-
-    grad_block(1, x + 2)
-    gred[1].far()
+            xsum[n, i] = ored[n].total(i).astype(BF16)
+            for kk in range(2):
+                send_if(
+                    always, xsum.at[n, i, pl.ds(kk * 96, 96)], zr.at[n, h], s_oz[n] + h,
+                    2 * k + i, kk, y, zl,
+                )
+
+    s_gz, s_gr = [new(2), new(2)], [new(4), new(4)]
+
+    def grad_zl(n, i):
+        for kk in range(2):
+            gsum[n, i, kk] = gred[n][i].total(kk)
+        gs[n, i] = gsum[n, i, 1 - zl].astype(BF16)
+        send(gs.at[n, i], gz.at[n, i], s_gz[n] + i, zpeer)
+
+    def grad_home(n, i):
+        got(gz.at[n, i], s_gz[n] + i)
+        gfin[n, i] = (gsum[n, i, zl] + gz[n, i].astype(F32)).astype(BF16)
+        for p in range(2):
+            plane = lax.rem(zl + 1 - p, 2)
+            if n == 0:
+                send_if(
+                    always, gfin.at[0, i], gu_out.at[zl, quarter, lanes(lax.rem(y, 2))],
+                    s_gr[0] + 2 * (1 - p) + lax.rem(y, 2), h, y // 2, 2 * k + i, plane,
+                )
+            else:
+                send_if(
+                    always, gfin.at[1, i], gd_out.at[quarter, lanes(y)],
+                    s_gr[1] + y, 2 * k + i, zl, h, plane,
+                )
+
+    back = [
+        Gather(lambda i, q: gu_out.at[:, rows(lax.rem(q, 4) * 80, 80), pl.ds(i * 640, 640)], "x"),
+        Gather(lambda i, q: gd_out.at[rows(lax.rem(q, 4) * 80, 80), pl.ds(i * 1280, 1280)], "x"),
+    ]
+
+    def back_first(n):
+        for i in range(2):
+            if n == 0:
+                got(gu_out.at[zl, quarter, pl.ds(i * 640, 640)], s_gr[0] + i)
+                got(gu_out.at[1 - zl, quarter, pl.ds(i * 640, 640)], s_gr[0] + 2 + i)
+            else:
+                for j in range(2):
+                    got(gd_out.at[quarter, pl.ds((2 * i + j) * 640, 640)], s_gr[1] + 2 * i + j)
+            back[n].first(i)
+
+    s_of = [new(1), new(1)]
+
+    def out_last(n):
+        total = jnp.zeros((96, 640), F32)
+        for a in range(4):
+            got(zr.at[n, a], s_oz[n] + a)
+            total = total + zr[n, a].astype(F32)
+        mine, theirs = split_lanes(total)
+        osend[n] = theirs
+        send(osend.at[n], orecv.at[n], s_of[n], partner)
+        if n == 0:
+            o_out[rows(k * 96, 96)] = (mine + bd_in[...]).astype(BF16)
+        else:
+            gi_out[rows(k * 96, 96)] = mine.astype(BF16)
+
+    tag[1][0].finish()
+    transpose(1, 0)
+    grad_start(1, 0)
+    for kk in range(2):
+        tag[1][1].forward(kk)
+    wag[1].finish()
     out_block(0, y + 2)
     ored[0].far()
-    grad_block(1, x + 1)
-    grad_block(1, x + 3)
-    gred[1].near()
-    out_block(0, y + 1)
-    out_block(0, y + 3)
-    ored[0].near()
+    grad_middle(1, 0)
+    tag[1][1].finish()
+    hps[1] = hidden(1, other_rows)
+    send(hps.at[1], hpr.at[1], s_hp[1], partner)
+    transpose(1, 1)
+    grad_start(1, 1)
     d_own = hidden(1, own_rows)
     got(hpr.at[1], s_hp[1])
     dhid[own_rows] = ((d_own + hpr[1]) * slope[...]).astype(BF16)
     send(dhid.at[own_rows], dhid.at[own_rows], s_act[1], partner)
-    grad_block(1, x)
-    gred[1].middle()
+    out_block(0, y + 1)
+    out_block(0, y + 3)
+    ored[0].near()
+    grad_zl(1, 0)
+    grad_middle(1, 1)
     got(dhid.at[other_rows], s_act[1])
-    grad_block(0, x + 2)
-    gred[0].far()
+    grad_start(0, 0)
     ored[0].middle()
+    grad_home(1, 0)
+    grad_start(0, 1)
+    grad_zl(1, 1)
     out_block(1, y + 2)
     ored[1].far()
-    grad_block(0, x + 1)
-    grad_block(0, x + 3)
-    gred[0].near()
+    grad_middle(0, 0)
     out_block(1, y + 1)
     out_block(1, y + 3)
     ored[1].near()
-    grad_block(0, x)
+    grad_home(1, 1)
+    grad_middle(0, 1)
     out_block(0, y)
     out_block(1, y)
-
+    grad_zl(0, 0)
+    ored[1].middle()
+    grad_zl(0, 1)
+    out_z(0)
     ones = jnp.ones((16, 768), BF16)
     terms = [nn(ones, dhid[...]), nn(ones, full[1, 0]), nn(ones, full[1, 1])]
     bt[...] = jnp.zeros_like(bt)
@@ -367,78 +498,10 @@
             if (a, b) != (0, 0):
                 send(bt, br.at[dep], s_bt + a * 2 + b, dep_at(a, b))
 
-    s_oz = [new(4), new(4)]
-
-    def out_z(n):
-        for i in range(2):
-            xsum[n, i] = ored[n].total(i).astype(BF16)
-            for kk in range(2):
-                send_maybe(
-                    xsum.at[n, i, pl.ds(kk * 96, 96)], zr.at[n, h], s_oz[n] + h, 2 * k + i, kk, y
-                )
-
-    s_gz, s_gr = [new(2), new(2)], [new(2), new(4)]
-
-    def grad_zl(n):
-        for i in range(2):
-            gz[n, 0, i] = gred[n].total(i).astype(BF16)
-            send(gz.at[n, 0, i], gz.at[n, 1, i], s_gz[n] + i, zpeer)
-
-    def grad_home(n):
-        for i in range(2):
-            got(gz.at[n, 1, i], s_gz[n] + i)
-            gfin[n, i] = (gz[n, 0, i].astype(F32) + gz[n, 1, i].astype(F32)).astype(BF16)
-            if n == 0:
-                lanes = pl.ds(pl.multiple_of(lax.rem(y, 2) * 640, 128), 640)
-                send_maybe(
-                    gfin.at[0, i], gu_out.at[:, quarter, lanes],
-                    s_gr[0] + lax.rem(y, 2), h, y // 2, 2 * k + i,
-                )
-            else:
-                lanes = pl.ds(pl.multiple_of(y * 640, 128), 640)
-                for kk in range(2):
-                    send_maybe(
-                        gfin.at[1, i, kk], gd_out.at[quarter, lanes], s_gr[1] + y, 2 * k + i, kk, h
-                    )
-
-    back = [
-        Gather(lambda i, q: gu_out.at[:, rows(lax.rem(q, 4) * 80, 80), pl.ds(i * 640, 640)], "x"),
-        Gather(lambda i, q: gd_out.at[rows(lax.rem(q, 4) * 80, 80), pl.ds(i * 1280, 1280)], "x"),
-    ]
-
-    def back_first(n):
-        for i in range(2):
-            if n == 0:
-                got(gu_out.at[:, quarter, pl.ds(i * 640, 640)], s_gr[0] + i)
-            else:
-                for j in range(2):
-                    got(gd_out.at[quarter, pl.ds((2 * i + j) * 640, 640)], s_gr[1] + 2 * i + j)
-            back[n].first(i)
-
-    s_of = [new(1), new(1)]
-
-    def out_last(n):
-        total = jnp.zeros((96, 640), F32)
-        for a in range(4):
-            got(zr.at[n, a], s_oz[n] + a)
-            total = total + zr[n, a].astype(F32)
-        mine, theirs = split_lanes(total)
-        osend[n] = theirs
-        send(osend.at[n], orecv.at[n], s_of[n], partner)
-        if n == 0:
-            o_out[rows(k * 96, 96)] = (mine + bd_in[...]).astype(BF16)
-        else:
-            gi_out[rows(k * 96, 96)] = mine.astype(BF16)
-
-    grad_zl(1)
-    gred[0].middle()
-    ored[1].middle()
-    grad_home(1)
-    out_z(0)
-    grad_zl(0)
     back_first(1)
+    grad_home(0, 0)
+    grad_home(0, 1)
     out_z(1)
-    grad_home(0)
 
     for a in range(4):
         for b in range(2):
@@ -495,6 +558,7 @@
     scratch = [
         ((2, 96, 320), BF16),
         ((2, 96, 640), BF16),
+        ((4, 80, 640), BF16),
         ((8, 1280), F32),
         ((8, 1280), F32),
         ((2, 2, 768, 640), BF16),
@@ -516,8 +580,10 @@
         ((2, 2, 2, 320, 640), BF16),
         ((2, 2, 2, 80, 640), BF16),
         ((2, 2, 2, 2, 80, 640), BF16),
-        ((2, 2, 2, 2, 80, 640), BF16),
-        ((2, 2, 2, 80, 640), BF16),
+        ((2, 2, 2, 80, 640), F32),
+        ((2, 2, 80, 640), BF16),
+        ((2, 2, 80, 640), BF16),
+        ((2, 2, 80, 640), BF16),
         ((16, 128), F32),
         ((8, 16, 128), F32),
         ((4, 16, 128), F32),

time: 171 us -> 144 us (0.84)
  the two profiles are of different devices: /device:TPU:88 before, /device:TPU:1 now
where the time goes in v3:
time: 144 us; the launch traced here: 142 us
  Pallas kernels  130 us (90%)
  local copies, waits for them, and re-layouts  11.6 us (8%)
    pallas_call x1, Pallas kernels, per_device(): pl.pallas_call(lambda *refs: kernel(scale, *refs), name='mlp_block', out_...  130 us
    unnamed x6, local copies, waits for them, and re-layouts  7.16 us

profile of v3, /device:TPU:1, one launch (start us, length us, event | category | flops | bytes accessed | tf_op | source)
XLA Modules:
  0.0 142.3 jit_solution(12725498519899369176)
XLA Ops:
  0.7 1.2 reshape.31.refs_4_
  1.9 1.3 reshape.30.refs_2_
  3.2 130.0 %mlp_block.1 = (bf16[192,320]{1,0:T(8,128)(2,1)}, bf16[192,320]{1,0:T(8,128)(2,1)}, bf16[2,320,1280]{2,1,0:T(8,128)(2,1)}, bf16[320,2560]{1,0:T(8,128)(2,1)}, f32[16,128]{1,0:T(8,128)}, /*index=5*/f32[16,128]{1,0:T(8,128)}) custom-call(bf16[192,320]{1,0:T(8,128)(2,1)} %refs_0_.1, bf16[2,320,1280]{2,1,0:T(8,128)(2,1)} %bitcast.10, ...), custom_call_target="tpu_custom_call" | custom-call | flops 7549747200 | bytes 12582912 | tf_op jit(solution)/shard_map/mlp_block/pallas_call | solution.py:592
  133.2 1.3 slice_bitcast_fusion
  134.5 0.6 dynamic_slice.5
  135.2 1.6 %copy.16 = bf16[192,320]{1,0:T(8,128)(2,1)} copy(bf16[192,320]{1,0:T(8,128)(2,1)} %get-tuple-element.26) | data formatting | bytes 245760
  136.7 1.6 %copy.17 = bf16[192,320]{1,0:T(8,128)(2,1)} copy(bf16[192,320]{1,0:T(8,128)(2,1)} %get-tuple-element.27) | data formatting | bytes 245760
  138.3 0.0 copy-start
  138.3 2.8 %copy.18 = bf16[640,1280]{1,0:T(8,128)(2,1)} copy(bf16[640,1280]{1,0:T(8,128)(2,1)} %bitcast.9) | data formatting | bytes 3276800
  141.2 0.0 copy-done
  141.2 1.2 copy.19
Async XLA Ops:
  138.3 2.8 %copy-start = (bf16[320,2560]{1,0:T(8,128)(2,1)S(1)}, bf16[320,2560]{1,0:T(8,128)(2,1)}, u32[]{:S(2)}) copy-start(bf16[320,2560]{1,0:T(8,128)(2,1)} %get-tuple-element.16) | copy-start | bytes 4915204

commit v4 on v3

--- a/solution.py
+++ b/solution.py
@@ -37,7 +37,7 @@
     scale,
     tok, wu_in, bu_in, wd_in, bd_in, grad,
     o_out, gi_out, gu_out, gd_out, bu_out, bd_out,
-    xr, piece, wq, bb, bbr,
+    xo, xr, bu, bd, piece, wq, bb, bbr,
     full, wts, full_t,
     hps, hpr, hpo, slope, act, dhid,
     part, ra, rb, xsum, zr, osend, orecv,
@@ -69,6 +69,20 @@
     partner = (h * 2 + 1 - k, y, dep)
     zpeer = dep_at(0, 1)
 
+    local = [
+        pltpu.make_async_copy(src, dst, sems.at[n])
+        for n, (src, dst) in enumerate(
+            (
+                (bu_in, bu),
+                (tok.at[rows(k * 96, 96)], xo.at[0]),
+                (grad.at[rows(k * 96, 96)], xo.at[1]),
+                (bd_in, bd),
+            )
+        )
+    ]
+    for copy in local:
+        copy.start()
+
     bar = pltpu.get_barrier_semaphore()
     fixed = [partner, z_at(1), z_at(3)] + [y_at(a) for a in (1, 2, 3)]
     fixed += [dep_at(a, b) for a in range(4) for b in range(2) if (a, b) != (0, 0)]
@@ -95,7 +109,7 @@
             count = count + greet(h, y // 2, 2 * k + a, b)
     pl.semaphore_wait(bar, count)
 
-    used = [0]
+    used = [len(local)]
     sent = []
 
     def new(n=1):
@@ -243,7 +257,10 @@
     for a in range(4):
         y_to = lax.rem(y + a, 4)
         send_if(always, wd_in.at[quarter, lanes(y_to)], wq.at[y], s_wq + a, h, k, y_to, zl)
-    bb[...] = jnp.broadcast_to(bu_in[...], bb.shape)
+    for copy in local:
+        copy.wait()
+    bb[...] = jnp.broadcast_to(bu[...].reshape(1, 1280), bb.shape)
+    bd_row = bd[...].reshape(1, 320)
     s_bb = new(1)
     send(bb, bbr, s_bb, partner)
 
@@ -254,9 +271,9 @@
     def part_of(n, i, kk):
         return full.at[n, i, rows(y * 192 + kk * 96, 96)]
 
-    def send_piece(n, src):
+    def send_piece(n):
         got(xr.at[n], s_x + n)
-        piece[n] = pair_lanes(src[rows(k * 96, 96), :], xr[n])
+        piece[n] = pair_lanes(xo[n], xr[n])
         dst = part_of(n, hi, k)
         sem = s_piece[n] + hi * 2 + k
         for a in (1, 3):
@@ -282,7 +299,7 @@
         got_piece(n, i, kk)
         tag[n][i].first(kk)
 
-    send_piece(0, tok)
+    send_piece(0)
     for i in range(2):
         got(wts.at[0, i, :, quarter], s_w[0] + i)
         wag[0].first(i)
@@ -296,7 +313,7 @@
     for i in range(2):
         for kk in range(2):
             over_y(0, i, kk)
-    send_piece(1, grad)
+    send_piece(1)
     for i in range(2):
         wag[0].forward(i)
     for i in range(2):
@@ -334,6 +351,8 @@
     for kk in range(2):
         tag[1][0].forward(kk)
     over_y(1, 1, 1)
+    for i in range(2):
+        wag[1].forward(i)
     got(bbr, s_bb)
     low = jnp.where(k == y // 2, bb[0:1], bbr[0:1])
     bias = jnp.where(lax.rem(y, 2) == 0, low[:, :640], low[:, 640:])
@@ -344,8 +363,6 @@
     send(act.at[own_rows], act.at[own_rows], s_act[0], partner)
     for i in range(2):
         transpose(0, i)
-    for i in range(2):
-        wag[1].forward(i)
     got(act.at[other_rows], s_act[0])
 
     ored = [Reduce(token_view(part.at[n]), ra.at[n], rb.at[n], "y") for n in range(2)]
@@ -438,7 +455,7 @@
         osend[n] = theirs
         send(osend.at[n], orecv.at[n], s_of[n], partner)
         if n == 0:
-            o_out[rows(k * 96, 96)] = (mine + bd_in[...]).astype(BF16)
+            o_out[rows(k * 96, 96)] = (mine + bd_row).astype(BF16)
         else:
             gi_out[rows(k * 96, 96)] = mine.astype(BF16)
 
@@ -451,6 +468,9 @@
     out_block(0, y + 2)
     ored[0].far()
     grad_middle(1, 0)
+    out_block(0, y + 1)
+    out_block(0, y + 3)
+    ored[0].near()
     tag[1][1].finish()
     hps[1] = hidden(1, other_rows)
     send(hps.at[1], hpr.at[1], s_hp[1], partner)
@@ -460,31 +480,23 @@
     got(hpr.at[1], s_hp[1])
     dhid[own_rows] = ((d_own + hpr[1]) * slope[...]).astype(BF16)
     send(dhid.at[own_rows], dhid.at[own_rows], s_act[1], partner)
-    out_block(0, y + 1)
-    out_block(0, y + 3)
-    ored[0].near()
+    ored[0].middle()
     grad_zl(1, 0)
     grad_middle(1, 1)
     got(dhid.at[other_rows], s_act[1])
     grad_start(0, 0)
-    ored[0].middle()
+    out_block(1, y + 2)
+    ored[1].far()
     grad_home(1, 0)
     grad_start(0, 1)
     grad_zl(1, 1)
-    out_block(1, y + 2)
-    ored[1].far()
-    grad_middle(0, 0)
     out_block(1, y + 1)
     out_block(1, y + 3)
     ored[1].near()
+    grad_middle(0, 0)
+    out_block(0, y)
     grad_home(1, 1)
     grad_middle(0, 1)
-    out_block(0, y)
-    out_block(1, y)
-    grad_zl(0, 0)
-    ored[1].middle()
-    grad_zl(0, 1)
-    out_z(0)
     ones = jnp.ones((16, 768), BF16)
     terms = [nn(ones, dhid[...]), nn(ones, full[1, 0]), nn(ones, full[1, 1])]
     bt[...] = jnp.zeros_like(bt)
@@ -497,12 +509,19 @@
         for b in range(2):
             if (a, b) != (0, 0):
                 send(bt, br.at[dep], s_bt + a * 2 + b, dep_at(a, b))
-
+    grad_zl(0, 0)
+    ored[1].middle()
+    grad_zl(0, 1)
+    out_block(1, y)
     back_first(1)
     grad_home(0, 0)
     grad_home(0, 1)
+    out_z(0)
     out_z(1)
-
+    for i in range(2):
+        back[1].forward(i)
+
+    back_first(0)
     for a in range(4):
         for b in range(2):
             if (a, b) != (0, 0):
@@ -518,21 +537,21 @@
     s_pb = new(1)
     send(yb.at[y], pb, s_pb, partner)
 
-    for i in range(2):
-        back[1].forward(i)
-    back_first(0)
     out_last(0)
     for i in range(2):
         back[0].forward(i)
     out_last(1)
     got(orecv.at[0], s_of[0])
-    o_out[rows((1 - k) * 96, 96)] = (orecv[0] + bd_in[...]).astype(BF16)
+    o_out[rows((1 - k) * 96, 96)] = (orecv[0] + bd_row).astype(BF16)
     for a in range(1, 4):
         got(yb.at[lax.rem(y + 4 - a, 4)], s_yb + a)
     got(pb, s_pb)
-    bu_out[0:5] = yb[2 * k][0:5]
-    bu_out[5:10] = yb[2 * k + 1][0:5]
-    bd_out[0:10] = jnp.where(k == hh, yb[y][5:15], pb[5:15])
+    wide = [yb[2 * k + j][n : n + 1] for j in range(2) for n in range(5)]
+    bu_out[...] = jnp.concatenate(wide, axis=1).astype(BF16).reshape(1280)
+    from_tile = jnp.where(k == hh, yb[y], pb[...])
+    wide = jnp.concatenate([from_tile[n : n + 1] for n in range(5, 15)], axis=1)
+    wide = jnp.where(hi == 0, wide[:, :640], wide[:, 640:])
+    bd_out[...] = jnp.where(k == 0, wide[:, :320], wide[:, 320:]).astype(BF16).reshape(320)
     got(orecv.at[1], s_of[1])
     gi_out[rows((1 - k) * 96, 96)] = orecv[1].astype(BF16)
     back[1].finish()
@@ -548,6 +567,17 @@
                 copy.wait_send()
 
     assert used[0] <= N_SEMS, used[0]
+
+
+def write_back(*refs):
+    sems = refs[-1]
+    copies = [
+        pltpu.make_async_copy(refs[n], refs[6 + n], sems.at[n]) for n in range(6)
+    ]
+    for copy in copies:
+        copy.start()
+    for copy in copies:
+        copy.wait()
 
 
 def per_device(tokens, up_weight, up_bias, down_weight, down_bias, out_grad):
@@ -557,6 +587,9 @@
     hbm = pl.BlockSpec(memory_space=pl.ANY)
     scratch = [
         ((2, 96, 320), BF16),
+        ((2, 96, 320), BF16),
+        ((1280,), F32),
+        ((320,), F32),
         ((2, 96, 640), BF16),
         ((4, 80, 640), BF16),
         ((8, 1280), F32),
@@ -593,37 +626,41 @@
         lambda *refs: kernel(scale, *refs),
         name="mlp_block",
         out_shape=[
-            jax.ShapeDtypeStruct((192, 320), BF16),
-            jax.ShapeDtypeStruct((192, 320), BF16),
-            jax.ShapeDtypeStruct((2, 320, 1280), BF16),
-            jax.ShapeDtypeStruct((320, 2560), BF16),
-            jax.ShapeDtypeStruct((16, 128), F32),
-            jax.ShapeDtypeStruct((16, 128), F32),
+            pltpu.VMEM((192, 320), BF16),
+            pltpu.VMEM((192, 320), BF16),
+            pltpu.VMEM((2, 320, 1280), BF16),
+            pltpu.VMEM((320, 2560), BF16),
+            pltpu.VMEM((1280,), BF16),
+            pltpu.VMEM((320,), BF16),
         ],
-        in_specs=[vmem, hbm, vmem, hbm, vmem, vmem],
+        in_specs=[hbm] * 6,
         out_specs=[vmem] * 6,
         scratch_shapes=[pltpu.VMEM(*s) for s in scratch] + [pltpu.SemaphoreType.DMA((N_SEMS,))],
         compiler_params=pltpu.CompilerParams(
-            collective_id=0, has_side_effects=True, vmem_limit_bytes=56 << 20
+            collective_id=0, has_side_effects=True, vmem_limit_bytes=44 << 20
         ),
         cost_estimate=pl.CostEstimate(
             flops=6 * 2 * 768 * 1280 * 640, bytes_accessed=12 << 20, transcendentals=384 * 640
         ),
     )(
-        tokens,
-        up_weight.reshape(2, 320, 1280),
-        up_bias.reshape(1, 1280),
-        down_weight.T,
-        down_bias.reshape(1, 320),
-        out_grad,
+        *[
+            pltpu.with_memory_space_constraint(a, pltpu.HBM)
+            for a in (
+                tokens, up_weight.reshape(2, 320, 1280), up_bias, down_weight.T, down_bias, out_grad
+            )
+        ]
     )
-    layer_out, grad_in, grad_up, grad_down, bu, bd = out
-    row = lax.axis_index("row")
-    grad_up_bias = bu[:10].reshape(1280).astype(BF16)
-    start = lax.rem(row // 2, 2) * 640 + lax.rem(row, 2) * 320
-    grad_down_bias = lax.dynamic_slice(bd[:10].reshape(1280), (start,), (320,)).astype(BF16)
-    grad_up = grad_up.reshape(640, 1280)
-    return (layer_out, grad_in, grad_up, grad_up_bias, grad_down.T, grad_down_bias)
+    layer_out, grad_in, grad_up, grad_down, bu, bd = pl.pallas_call(
+        write_back,
+        name="write_back",
+        out_shape=[jax.ShapeDtypeStruct(a.shape, a.dtype) for a in out],
+        in_specs=[vmem] * 6,
+        out_specs=[hbm] * 6,
+        scratch_shapes=[pltpu.SemaphoreType.DMA((6,))],
+        compiler_params=pltpu.CompilerParams(vmem_limit_bytes=1 << 20),
+        cost_estimate=pl.CostEstimate(flops=0, bytes_accessed=8 << 20, transcendentals=0),
+    )(*[pltpu.with_memory_space_constraint(a, pltpu.VMEM) for a in out])
+    return (layer_out, grad_in, grad_up.reshape(640, 1280), bu, grad_down.T, bd)
 
 
 def solution(mesh):

time: 144 us -> 131 us (0.910)
  the two profiles are of different devices: /device:TPU:1 before, /device:TPU:65 now
where the time goes in v4:
time: 131 us
  Pallas kernels  130 us (99%)
    pallas_call x1, Pallas kernels, per_device(): pl.pallas_call(lambda *refs: kernel(scale, *refs), name='mlp_block', out_...  128 us

profile of v4, /device:TPU:65, one launch (start us, length us, event | category | flops | bytes accessed | tf_op | source)
XLA Modules:
  0.0 130.6 jit_solution(11451967925899183199)
XLA Ops:
  0.6 127.9 %mlp_block.1 = (bf16[192,320]{1,0:T(8,128)(2,1)S(1)}, bf16[192,320]{1,0:T(8,128)(2,1)S(1)}, bf16[2,320,1280]{2,1,0:T(8,128)(2,1)S(1)}, bf16[320,2560]{1,0:T(8,12...) custom-call(bf16[192,320]{1,0:T(8,128)(2,1)} %refs_0_.1, bf16[2,320,1280]{2,1,0:T(8,128)(2,1)} %bitcast.4, ...), custom_call_target="tpu_custom_call" | custom-call | flops 7549747200 | bytes 12582912 | tf_op jit(solution)/shard_map/mlp_block/pallas_call | solution.py:625
  128.6 1.9 %write_back.1 = (bf16[192,320]{1,0:T(8,128)(2,1)}, bf16[192,320]{1,0:T(8,128)(2,1)}, bf16[2,320,1280]{2,1,0:T(8,128)(2,1)}, bf16[320,2560]{1,0:T(8,128)(2,1)}, b...) custom-call(bf16[192,320]{1,0:T(8,128)(2,1)S(1)} %get-tuple-element.18.refs_0_, ...), custom_call_target="tpu_custom_call" | custom-call | bytes 8388608 | tf_op jit(solution)/shard_map/write_back/pallas_call | solution.py:653

commit v5 on v4

--- a/solution.py
+++ b/solution.py
@@ -241,6 +241,8 @@
         send(src.at[rows((1 - k) * 96, 96)], xr.at[n], s_x + n, partner)
     quarter = rows(x * 80, 80)
     always = k >= 0
+    near = jnp.where(hh == k, hi, 1 - hi)
+    order = [near, 1 - near]
 
     def lanes(n):
         return pl.ds(pl.multiple_of(n * 640, 128), 640)
@@ -265,8 +267,9 @@
     send(bb, bbr, s_bb, partner)
 
     s_piece = [new(4), new(4)]
-    to_right = [h == lax.rem(2 * k + i + 1, 4) for i in range(2)]
-    to_left = [h == lax.rem(2 * k + i + 3, 4) for i in range(2)]
+
+    def passes(i, kk):
+        return h == lax.rem(2 * k + i + (1, 3)[kk], 4)
 
     def part_of(n, i, kk):
         return full.at[n, i, rows(y * 192 + kk * 96, 96)]
@@ -282,21 +285,21 @@
 
     def pass_piece(n):
         for i in range(2):
-            for kk, only, a in ((0, to_right[i], 1), (1, to_left[i], 3)):
+            for kk, a in ((0, 1), (1, 3)):
+                only = passes(i, kk)
                 sem = s_piece[n] + i * 2 + kk
                 block = part_of(n, i, kk)
                 got_if(only, block, sem)
                 send_if(only, block, block, sem, lax.rem(h + a, 4), k, y, zl)
 
     def got_piece(n, i, kk):
-        only = (to_right, to_left)[kk][i]
-        got_if(jnp.logical_not(only), part_of(n, i, kk), s_piece[n] + i * 2 + kk)
+        got_if(jnp.logical_not(passes(i, kk)), part_of(n, i, kk), s_piece[n] + i * 2 + kk)
 
     wag = [Gather(chunk_view(wts.at[n]), "x") for n in range(2)]
-    tag = [[Gather(half_view(full.at[n], i), "y") for i in range(2)] for n in range(2)]
+    tag = [[Gather(half_view(full.at[n], i), "y") for i in order] for n in range(2)]
 
     def over_y(n, i, kk):
-        got_piece(n, i, kk)
+        got_piece(n, order[i], kk)
         tag[n][i].first(kk)
 
     send_piece(0)
@@ -304,15 +307,16 @@
         got(wts.at[0, i, :, quarter], s_w[0] + i)
         wag[0].first(i)
     pass_piece(0)
+    for kk in range(2):
+        over_y(0, 0, kk)
     for a in range(4):
         origin = lax.rem(y + 4 - a, 4)
         got(wq.at[origin], s_wq + a)
         send_if(
             always, wq.at[origin], wts.at[1, hi, k, quarter], s_w[1] + hi * 2 + k, origin, hh, y, zl
         )
-    for i in range(2):
-        for kk in range(2):
-            over_y(0, i, kk)
+    for kk in range(2):
+        over_y(0, 1, kk)
     send_piece(1)
     for i in range(2):
         wag[0].forward(i)
@@ -367,7 +371,7 @@
 
     ored = [Reduce(token_view(part.at[n]), ra.at[n], rb.at[n], "y") for n in range(2)]
     gred = [
-        [Reduce(chunk_half_view(gpart.at[n], i), ga.at[n, i], gb.at[n, i], "x") for i in range(2)]
+        [Reduce(chunk_half_view(gpart.at[n], i), ga.at[n, j], gb.at[n, j], "x") for j, i in enumerate(order)]
         for n in range(2)
     ]
 
@@ -377,7 +381,8 @@
         for i in range(2):
             part[n, i, block] = nt(left[block], weight(1 - n, i)).astype(BF16)
 
-    def grad_block(n, i, q):
+    def grad_block(n, j, q):
+        i = order[j]
         block = rows(lax.rem(q, 4) * 80, 80)
         right = dhid if n == 0 else act
         left = full_t[n, i, :, block].reshape(160, 768)
@@ -416,17 +421,18 @@
     def grad_home(n, i):
         got(gz.at[n, i], s_gz[n] + i)
         gfin[n, i] = (gsum[n, i, zl] + gz[n, i].astype(F32)).astype(BF16)
+        to = 2 * k + order[i]
         for p in range(2):
             plane = lax.rem(zl + 1 - p, 2)
             if n == 0:
                 send_if(
                     always, gfin.at[0, i], gu_out.at[zl, quarter, lanes(lax.rem(y, 2))],
-                    s_gr[0] + 2 * (1 - p) + lax.rem(y, 2), h, y // 2, 2 * k + i, plane,
+                    s_gr[0] + 2 * (1 - p) + lax.rem(y, 2), h, y // 2, to, plane,
                 )
             else:
                 send_if(
                     always, gfin.at[1, i], gd_out.at[quarter, lanes(y)],
-                    s_gr[1] + y, 2 * k + i, zl, h, plane,
+                    s_gr[1] + y, to, zl, h, plane,
                 )
 
     back = [
@@ -460,7 +466,7 @@
             gi_out[rows(k * 96, 96)] = mine.astype(BF16)
 
     tag[1][0].finish()
-    transpose(1, 0)
+    transpose(1, order[0])
     grad_start(1, 0)
     for kk in range(2):
         tag[1][1].forward(kk)
@@ -474,7 +480,7 @@
     tag[1][1].finish()
     hps[1] = hidden(1, other_rows)
     send(hps.at[1], hpr.at[1], s_hp[1], partner)
-    transpose(1, 1)
+    transpose(1, order[1])
     grad_start(1, 1)
     d_own = hidden(1, own_rows)
     got(hpr.at[1], s_hp[1])

time: 131 us -> 123 us (0.939)
  the two profiles are of different devices: /device:TPU:65 before, /device:TPU:1 now
where the time goes in v5:
time: 123 us; the launch traced here: 122 us
  Pallas kernels  121 us (98%)
    pallas_call x1, Pallas kernels, per_device(): pl.pallas_call(lambda *refs: kernel(scale, *refs), name='mlp_block', out_...  120 us

profile of v5, /device:TPU:1, one launch (start us, length us, event | category | flops | bytes accessed | tf_op | source)
XLA Modules:
  0.0 122.3 jit_solution(1251146589937598451)
XLA Ops:
  0.6 119.6 %mlp_block.1 = (bf16[192,320]{1,0:T(8,128)(2,1)S(1)}, bf16[192,320]{1,0:T(8,128)(2,1)S(1)}, bf16[2,320,1280]{2,1,0:T(8,128)(2,1)S(1)}, bf16[320,2560]{1,0:T(8,12...) custom-call(bf16[192,320]{1,0:T(8,128)(2,1)} %refs_0_.1, bf16[2,320,1280]{2,1,0:T(8,128)(2,1)} %bitcast.4, ...), custom_call_target="tpu_custom_call" | custom-call | flops 7549747200 | bytes 12582912 | tf_op jit(solution)/shard_map/mlp_block/pallas_call | solution.py:631
  120.3 1.9 %write_back.1 = (bf16[192,320]{1,0:T(8,128)(2,1)}, bf16[192,320]{1,0:T(8,128)(2,1)}, bf16[2,320,1280]{2,1,0:T(8,128)(2,1)}, bf16[320,2560]{1,0:T(8,128)(2,1)}, b...) custom-call(bf16[192,320]{1,0:T(8,128)(2,1)S(1)} %get-tuple-element.18.refs_0_, ...), custom_call_target="tpu_custom_call" | custom-call | bytes 8388608 | tf_op jit(solution)/shard_map/write_back/pallas_call | solution.py:659

commit v6 on v5

--- a/solution.py
+++ b/solution.py
@@ -518,11 +518,11 @@
     grad_zl(0, 0)
     ored[1].middle()
     grad_zl(0, 1)
-    out_block(1, y)
+    grad_home(0, 0)
     back_first(1)
-    grad_home(0, 0)
     grad_home(0, 1)
     out_z(0)
+    out_block(1, y)
     out_z(1)
     for i in range(2):
         back[1].forward(i)

time: 123 us -> 123 us (level)
  no operation moved by 1% of the time
where the time goes in v6:
time: 123 us
  Pallas kernels  122 us (99%)
    pallas_call x1, Pallas kernels, per_device(): pl.pallas_call(lambda *refs: kernel(scale, *refs), name='mlp_block', out_...  120 us

profile of v6, /device:TPU:1, one launch (start us, length us, event | category | flops | bytes accessed | tf_op | source)
XLA Modules:
  0.0 122.8 jit_solution(13091807977800552780)
XLA Ops:
  0.6 120.1 %mlp_block.1 = (bf16[192,320]{1,0:T(8,128)(2,1)S(1)}, bf16[192,320]{1,0:T(8,128)(2,1)S(1)}, bf16[2,320,1280]{2,1,0:T(8,128)(2,1)S(1)}, bf16[320,2560]{1,0:T(8,12...) custom-call(bf16[192,320]{1,0:T(8,128)(2,1)} %refs_0_.1, bf16[2,320,1280]{2,1,0:T(8,128)(2,1)} %bitcast.4, ...), custom_call_target="tpu_custom_call" | custom-call | flops 7549747200 | bytes 12582912 | tf_op jit(solution)/shard_map/mlp_block/pallas_call | solution.py:631
  120.7 1.9 %write_back.1 = (bf16[192,320]{1,0:T(8,128)(2,1)}, bf16[192,320]{1,0:T(8,128)(2,1)}, bf16[2,320,1280]{2,1,0:T(8,128)(2,1)}, bf16[320,2560]{1,0:T(8,128)(2,1)}, b...) custom-call(bf16[192,320]{1,0:T(8,128)(2,1)S(1)} %get-tuple-element.18.refs_0_, ...), custom_call_target="tpu_custom_call" | custom-call | bytes 8388608 | tf_op jit(solution)/shard_map/write_back/pallas_call | solution.py:659
